TPU v7x, 256 devices: a whole 4x4x8 slice. The times are simulated.
256 devices in a mesh: gx: 16 (over x, y_hi, core), gy: 16 (over z, y_lo).
Axes of the slice: x: 4, y: 4 (y_hi: 2, y_lo: 2; y = y_hi * 2 + y_lo), z: 8, core: 2. Of those that a mesh axis runs over, the one named last changes fastest.
Arguments:
- scalars: float32 [2, 384, 512, 128], P(None, 'gx', 'gy'), may hold values from -10 to 10
- east_wind: float32 [384, 512, 128], P('gx', 'gy'), may hold values from -1 to 1
- north_wind: float32 [384, 512, 128], P('gx', 'gy'), may hold values from -1 to 1
- up_wind: float32 [384, 512, 128], P('gx', 'gy'), may hold values from -1 to 1
- diffusivity: float32 [384, 512, 128], P('gx', 'gy'), may hold values from 0.05 to 300
- target_profile: float32 [2, 128], replicated, may hold values from -6 to 6
Outputs:
- updated: float32 [2, 384, 512, 128], P(None, 'gx', 'gy')
All inputs are finite; a program needn't handle non-finite values.
Results may differ from a plain program's by a relative error of at most 0.0003.
Values sent between devices are 32-bit elements; how exact they have to be, the bound alone decides.
A program may use at most 64 MiB of HBM per device.

v0:
```python
import functools

import jax
import jax.numpy as jnp
from jax import lax
from jax.experimental import pallas as pl
from jax.experimental.pallas import tpu as pltpu
from jax.sharding import PartitionSpec as P

STEP = 0.3
RELAX = 0.5
EPSILON = 1e-06
EPS = 0.75 * EPSILON
EPS2 = EPS * EPS

CX, CY, NZ = 24, 32, 128
H = 3
XROWS = (CX + 2 * H) * CY
YROWS = (CY + 2 * H) * CX
CELLS = CX * CY
TILES = CELLS // 128
GROUP = 4
ZROWS = 96
PART = 24
LEVELS = 6 * PART
PLACES = (0, 1, 3)
MESH = pl.DeviceIdType.MESH


def cell(dm, em, dp, ep):
    g = dp - dm
    b = (g * g + EPS) + ep * dm
    g2 = g + g
    left = b - g2 * em
    right = b + g2 * ep
    return g, left * left, b * b, right * right


def face(u, total, g_low, g_high, t_low, t_mid, t_high, r2, r1, c1, c0, l0, l1):
    pos = u > 0.0
    b0 = jnp.where(pos, r2, l1)
    b1 = jnp.where(pos, c1, c0)
    b2 = jnp.where(pos, l0, r1)
    gs = jnp.where(pos, g_low, g_high)
    ts = jnp.where(pos, t_low, t_high)
    b0 = 3.0 * b0
    c2 = b2 + b2
    num = b1 * (c2 * ts + b0 * t_mid)
    den = b1 * (b2 + b0) + b0 * c2
    part = num * pl.reciprocal(den, approx=True)
    return u * (3.0 * total - gs) - jnp.abs(u) * part


def march(load_f, load_u, first, last):
    f, d, q, t = {}, {}, {}, {}

    def get_f(i):
        if i not in f:
            f[i] = load_f(i)
        return f[i]

    def get_d(i):
        if i not in d:
            diff = get_f(i) - get_f(i - 1)
            d[i] = (diff, 0.75 * diff)
        return d[i]

    def get_q(i):
        if i not in q:
            q[i] = cell(*get_d(i), *get_d(i + 1))
        return q[i]

    def get_t(i):
        if i not in t:
            t[i] = get_q(i)[0] - get_q(i - 1)[0]
        return t[i]

    out = []
    for j in range(first, last + 1):
        lo2, lo1, hi0, hi1 = get_q(j - 2), get_q(j - 1), get_q(j), get_q(j + 1)
        out.append(
            face(
                load_u(j), get_f(j - 1) + get_f(j), lo1[0], hi0[0], get_t(j - 1), get_t(j), get_t(j + 1),
                lo2[3], lo1[3], lo1[2], hi0[2], hi0[1], hi1[1],
            )
        )
    return out


def shifted_z(f, lane):
    below, below2, above = pltpu.roll(f, 1, 1), pltpu.roll(f, 2, 1), pltpu.roll(f, NZ - 1, 1)
    d = jnp.where(lane == 0, 0.0, f - below)
    d_low = jnp.where(lane <= 1, 0.0, below - below2)
    d_high = jnp.where(lane == NZ - 1, 0.0, above - f)
    g, left, mid, right = cell(d, 0.75 * d, d_high, 0.75 * d_high)
    g_low = d - d_low
    t = g - g_low
    return (
        f + below, g_low, g, pltpu.roll(t, 1, 1), t, pltpu.roll(t, NZ - 1, 1), pltpu.roll(right, 2, 1),
        pltpu.roll(right, 1, 1), pltpu.roll(mid, 1, 1), mid, left, pltpu.roll(left, NZ - 1, 1),
    )


def flux_z(u, parts, lane):
    total, g_low, g, t_low, t, t_high, r2, r1, c1, c0, l0, l1 = parts
    last = lane == NZ - 1
    t_high = jnp.where(last, -g, t_high)
    r2 = jnp.where(lane == 1, EPS2, r2)
    l1 = jnp.where(last, EPS2, l1)
    return face(u, total, g_low, g, t_low, t, t_high, r2, r1, c1, c0, l0, l1)


def digits(n):
    out, stride = [], 1
    while stride < n:
        radix = min(4, n // stride)
        out.append((stride, radix))
        stride *= radix
    return out


def kernel(
    n_x, n_y,
    scal, east, north, upw, diff, target, adv, shift, im, av, cp,
    xs, bs, ys, zs, fz, fr, tx, ty, ex, ny, nraw, uz, kd, tg, fk, es, aro, ari,
    lsem, hsend, hrecv, wsend, wrecv, asend, arecv,
):
    mx, my = lax.axis_index("gx"), lax.axis_index("gy")
    x_up, x_dn = lax.rem(mx + 1, n_x), lax.rem(mx + n_x - 1, n_x)
    y_up, y_dn = lax.rem(my + 1, n_y), lax.rem(my + n_y - 1, n_y)
    plan = [("x", d) for d in digits(n_x)] + [("y", d) for d in digits(n_y)]
    rounds = len(plan)

    def partner(r, k):
        axis, (stride, radix) = plan[r]
        me = mx if axis == "x" else my
        digit = lax.rem(lax.div(me, stride), radix)
        other = me + stride * (lax.rem(digit + k, radix) - digit)
        return (other, my) if axis == "x" else (mx, other)

    loads = [
        pltpu.make_async_copy(scal.at[0], xs.at[0, 0, pl.ds(H * CY, CELLS)], lsem.at[0]),
        pltpu.make_async_copy(scal.at[1], xs.at[0, 1, pl.ds(H * CY, CELLS)], lsem.at[1]),
        pltpu.make_async_copy(north, nraw, lsem.at[2]),
        pltpu.make_async_copy(east, ex.at[pl.ds(0, CELLS)], lsem.at[3]),
        pltpu.make_async_copy(diff, kd, lsem.at[4]),
        pltpu.make_async_copy(upw, uz, lsem.at[5]),
        pltpu.make_async_copy(target, tg, lsem.at[6]),
        pltpu.make_async_copy(scal, bs, lsem.at[7]),
    ]
    for load in loads:
        load.start()

    barrier = pltpu.get_barrier_semaphore()
    peers = [(x_up, my), (x_dn, my), (mx, y_up), (mx, y_dn)] + [
        partner(r, k) for r in range(rounds) for k in range(1, plan[r][1][1])
    ]
    for peer in peers:
        pl.semaphore_signal(barrier, inc=1, device_id=peer, device_id_type=MESH)

    def halo(t, way, plane=None):
        st, s = lax.div(t, 2), lax.rem(t, 2)
        size = CY if way < 2 else CX
        buffer, length = (xs, CX) if way < 2 else (ys, CY)
        to = ((x_up, my), (x_dn, my), (mx, y_up), (mx, y_dn))[way]
        source, target_row = ((length, 0), (H, length + H))[way % 2]
        first, count = (0, H) if plane is None else (plane, 1)
        return pltpu.make_async_remote_copy(
            src_ref=buffer.at[st, s, pl.ds((source + first) * size, count * size)],
            dst_ref=buffer.at[st, s, pl.ds((target_row + first) * size, count * size)],
            send_sem=hsend.at[t, way], recv_sem=hrecv.at[t, way], device_id=to, device_id_type=MESH,
        )

    def send_halos(t, ways):
        for plane in range(H):
            for way in ways:
                halo(t, way, plane).start()

    def exchange(r):
        return [
            pltpu.make_async_remote_copy(
                src_ref=aro.at[r], dst_ref=ari.at[r, k - 1], send_sem=asend.at[r, k - 1],
                recv_sem=arecv.at[r, k - 1], device_id=partner(r, k), device_id_type=MESH,
            )
            for k in range(1, plan[r][1][1])
        ]

    def send_sums(r):
        for copy in exchange(r):
            copy.start()

    def add_sums(r):
        total = aro[r]
        for k, copy in enumerate(exchange(r)):
            copy.wait_recv()
            total = total + ari[r, k]
        aro[r + 1] = total

    east_edge = pltpu.make_async_remote_copy(
        src_ref=ex.at[pl.ds(0, CY)], dst_ref=ex.at[pl.ds(CELLS, CY)], send_sem=wsend.at[0], recv_sem=wrecv.at[0],
        device_id=(x_dn, my), device_id_type=MESH,
    )
    north_edge = pltpu.make_async_remote_copy(
        src_ref=ny.at[pl.ds(0, CX)], dst_ref=ny.at[pl.ds(CELLS, CX)], send_sem=wsend.at[1], recv_sem=wrecv.at[1],
        device_id=(mx, y_dn), device_id_type=MESH,
    )

    def to_y(st, s, x, value):
        for i in range(CY // 8):
            ys[st, s, pl.ds((H + 8 * i) * CX + x, 8, stride=CX), :] = value[8 * i : 8 * i + 8]

    loads[0].wait()
    loads[1].wait()
    pl.semaphore_wait(barrier, len(peers))
    for s in range(2):
        send_halos(s, (0, 1))
    for s in range(2):

        def convert(g, total, s=s):
            values = [xs[0, s, pl.ds((H + g * GROUP + p) * CY, CY), :] for p in range(GROUP)]
            for p, value in enumerate(values):
                to_y(0, s, g * GROUP + p, value)
            return total + sum(values)

        total = lax.fori_loop(0, CX // GROUP, convert, jnp.zeros((CY, NZ), jnp.float32))
        aro[0, s : s + 1, :] = jnp.sum(total, axis=0, keepdims=True)
        send_halos(s, (2, 3))
    send_sums(0)

    loads[2].wait()

    def scale_north(g, _):
        values = [nraw[pl.ds((g * GROUP + p) * CY, CY), :] * (1.0 / 6.0) for p in range(GROUP)]
        for p, value in enumerate(values):
            for i in range(CY // 8):
                ny[pl.ds(8 * i * CX + g * GROUP + p, 8, stride=CX), :] = value[8 * i : 8 * i + 8]
        return 0

    lax.fori_loop(0, CX // GROUP, scale_north, 0)
    north_edge.start()
    loads[3].wait()

    def scale_east(g, _):
        rows = pl.ds(pl.multiple_of(g * GROUP * CY, CY), GROUP * CY)
        ex[rows, :] = ex[rows, :] * (1.0 / 6.0)
        return 0

    lax.fori_loop(0, CX // GROUP, scale_east, 0)
    east_edge.start()
    loads[5].wait()
    lane = lax.broadcasted_iota(jnp.int32, (8, NZ), 1)
    lane_all = lax.broadcasted_iota(jnp.int32, (GROUP * CY, NZ), 1)

    def scale_up(g, _):
        rows = pl.ds(pl.multiple_of(g * GROUP * CY, CY), GROUP * CY)
        uz[rows, :] = jnp.where(lane_all == 0, 0.0, uz[rows, :] * (1.0 / 6.0))
        return 0

    lax.fori_loop(0, CX // GROUP, scale_up, 0)

    loads[4].wait()
    loads[6].wait()
    loads[7].wait()
    for c in range(8):
        if c < TILES:
            levels = jnp.transpose(kd[pl.ds(c * 128, 128), :]) * STEP
        else:
            levels = jnp.zeros((NZ, 128), jnp.float32)
        fk[pl.ds(c, NZ, stride=8), :] = levels
    fk[pl.ds(0, 8), :] = jnp.zeros((8, 128), jnp.float32)
    fk[pl.ds(NZ * 8, (LEVELS - NZ + 1) * 8), :] = jnp.zeros(((LEVELS - NZ + 1) * 8, 128), jnp.float32)
    es[...] = jnp.zeros((8, 128), jnp.float32)

    def factor(part):
        base = pl.multiple_of(part * (PART * 8), 8)
        low = fk[pl.ds(base, 8), :]
        e = es[...]
        for i in range(PART):
            row = pl.ds(base + 8 * i, 8)
            above = fk[pl.ds(base + 8 * i + 8, 8), :]
            g = 1.0 + low * e
            inverse = pl.reciprocal(g + above, approx=True)
            e = g * inverse
            im[row, :] = inverse
            av[row, :] = low * inverse
            cp[row, :] = above * inverse
            low = above
        es[...] = e

    def x_faces(st, s, row, first, last):
        flux = march(
            lambda x: xs[st, s, pl.ds((H + x) * CY + row, 8), :],
            lambda x: ex[pl.ds(x * CY + row, 8), :],
            first, last,
        )
        for x in range(first, last):
            tx[pl.ds(x * CY + row, 8), :] = flux[x - first] - flux[x - first + 1]

    def y_faces(st, s, row, first, last):
        flux = march(
            lambda y: ys[st, s, pl.ds((H + y) * CX + row, 8), :],
            lambda y: ny[pl.ds(y * CX + row, 8), :],
            first, last,
        )
        for y in range(first, last):
            ty[pl.ds(row * CY + y, 8, stride=CY), :] = flux[y - first] - flux[y - first + 1]

    def z_faces(st, s):
        groups = CELLS // ZROWS

        def group(i, _):
            late = pl.multiple_of(lax.max(i - 1, 0) * ZROWS, ZROWS)
            now = pl.multiple_of(lax.min(i, groups - 1) * ZROWS, ZROWS)
            for v in range(ZROWS // 8):
                flux = flux_z(
                    uz[pl.ds(late + 8 * v, 8), :], [zs[part, 8 * v : 8 * v + 8, :] for part in range(12)], lane
                )
                fz[pl.ds(late + 8 * v, 8), :] = flux
                fr[pl.ds(late + 8 * v, 8), :] = pltpu.roll(flux, NZ - 1, 1)
            for v in range(ZROWS // 8):
                parts = shifted_z(xs[st, s, pl.ds(H * CY + now + 8 * v, 8), :], lane)
                for part in range(12):
                    zs[part, 8 * v : 8 * v + 8, :] = parts[part]
            return 0

        lax.fori_loop(0, groups + 1, group, 0)

    def columns(count, work):
        def block(i, _):
            work(pl.multiple_of(i * 8, 8))
            return 0

        lax.fori_loop(0, count, block, 0)

    def step(t, _):
        st, s = lax.div(t, 2), lax.rem(t, 2)
        factor(t)
        columns(CX // 8, lambda row: y_faces(st, s, row, H, CY - H))
        columns(CY // 8, lambda row: x_faces(st, s, row, H, CX - H))
        z_faces(st, s)
        for r, place in enumerate(PLACES[: rounds - 1]):

            @pl.when(t == place)
            def _(r=r):
                add_sums(r)
                send_sums(r + 1)


        @pl.when(t == 0)
        def _():
            north_edge.wait_recv()
            east_edge.wait_recv()

        halo(t, 2).wait_recv()
        halo(t, 3).wait_recv()
        columns(CX // 8, lambda row: (y_faces(st, s, row, 0, H), y_faces(st, s, row, CY - H, CY)))
        halo(t, 0).wait_recv()
        halo(t, 1).wait_recv()
        columns(CY // 8, lambda row: (x_faces(st, s, row, 0, H), x_faces(st, s, row, CX - H, CX)))
        coef = jnp.where(st == 0, STEP / 3.0, jnp.where(st == 1, STEP * 0.5, STEP)).astype(jnp.float32)

        def update(g, _):
            rows = pl.ds(pl.multiple_of(g * GROUP * CY, CY), GROUP * CY)
            value = bs[s, rows, :] + coef * (tx[rows, :] + ty[rows, :] + (fz[rows, :] - fr[rows, :]))
            xs[st + 1, s, pl.ds(pl.multiple_of((H + g * GROUP) * CY, CY), GROUP * CY), :] = value
            for p in range(GROUP):
                to_y(st + 1, s, g * GROUP + p, value[p * CY : (p + 1) * CY])
            return 0

        lax.fori_loop(0, CX // GROUP, update, 0)

        @pl.when(st < 2)
        def _():
            send_halos(t + 2, range(4))

        return 0

    lax.fori_loop(0, 6, step, 0)

    add_sums(rounds - 1)
    cells = float(n_x * CX * n_y * CY)
    shift[...] = RELAX * (aro[rounds] * (1.0 / cells) - tg[...])
    for s in range(2):
        adv[s] = xs[3, s, pl.ds(H * CY, CELLS), :]

    def drain(t, _):
        for way in range(4):
            halo(t, way).wait_send()
        return 0

    lax.fori_loop(0, 6, drain, 0)

    for r in range(rounds):
        for copy in exchange(r):
            copy.wait_send()
    east_edge.wait_send()
    north_edge.wait_send()


def solve(adv, shift, im, av, cp, out, rh, ob, osem):
    for s in range(2):
        for c in range(TILES):
            value = adv[s, pl.ds(c * 128, 128), :] - shift[s : s + 1, :]
            rh[s, pl.ds(c, NZ, stride=8), :] = jnp.transpose(value)

    zero = jnp.zeros((8, 128), jnp.float32)

    def forward(k8, carry):
        d0, d1 = carry
        base = pl.multiple_of(k8 * 64, 64)
        rows = [pl.ds(base + 8 * i, 8) for i in range(8)]
        data = [(im[r, :], av[r, :], rh[0, r, :], rh[1, r, :]) for r in rows]
        for i, (inverse, a, r0, r1) in enumerate(data):
            d0 = r0 * inverse + a * d0
            d1 = r1 * inverse + a * d1
            rh[0, rows[i], :] = d0
            rh[1, rows[i], :] = d1
        return d0, d1

    lax.fori_loop(0, NZ // 8, forward, (zero, zero))

    def backward(j8, carry):
        v0, v1 = carry
        base = pl.multiple_of((NZ // 8 - 1 - j8) * 64, 64)
        rows = [pl.ds(base + 56 - 8 * i, 8) for i in range(8)]
        data = [(cp[r, :], rh[0, r, :], rh[1, r, :]) for r in rows]
        for i, (c, r0, r1) in enumerate(data):
            v0 = r0 + c * v0
            v1 = r1 + c * v1
            rh[0, rows[i], :] = v0
            rh[1, rows[i], :] = v1
        return v0, v1

    lax.fori_loop(0, NZ // 8, backward, (zero, zero))
    stores = []
    for s in range(2):
        for c in range(TILES):
            rows = pl.ds(c * 128, 128)
            ob[s, rows, :] = jnp.transpose(rh[s, pl.ds(c, NZ, stride=8), :])
            store = pltpu.make_async_copy(ob.at[s, rows], out.at[s, rows], osem.at[s, c])
            store.start()
            stores.append(store)
    for store in stores:
        store.wait()


def in_hbm(value):
    return pltpu.with_memory_space_constraint(value, pltpu.HBM)


def body(n_x, n_y, scalars, east_wind, north_wind, up_wind, diffusivity, target_profile):
    rounds = len(digits(n_x)) + len(digits(n_y))
    hbm = pl.BlockSpec(memory_space=pltpu.HBM)
    f32 = jnp.float32
    vmem = pltpu.VMEM
    dma = pltpu.SemaphoreType.DMA
    resident = pl.BlockSpec(memory_space=pltpu.VMEM)
    columns = jax.ShapeDtypeStruct((LEVELS * 8, 128), f32)
    parts = pl.pallas_call(
        functools.partial(kernel, n_x, n_y),
        out_shape=[
            jax.ShapeDtypeStruct((2, CELLS, NZ), f32), jax.ShapeDtypeStruct((2, NZ), f32), columns, columns, columns,
        ],
        in_specs=[hbm] * 6,
        out_specs=[resident] * 5,
        scratch_shapes=[
            vmem((4, 2, XROWS, NZ), f32),
            vmem((2, CELLS, NZ), f32),
            vmem((4, 2, YROWS, NZ), f32),
            vmem((12, ZROWS, NZ), f32),
            vmem((CELLS, NZ), f32),
            vmem((CELLS, NZ), f32),
            vmem((CELLS, NZ), f32),
            vmem((CELLS, NZ), f32),
            vmem((CELLS + CY, NZ), f32),
            vmem((CELLS + CX, NZ), f32),
            vmem((CELLS, NZ), f32),
            vmem((CELLS, NZ), f32),
            vmem((CELLS, NZ), f32),
            vmem((2, NZ), f32),
            vmem(((LEVELS + 1) * 8, 128), f32),
            vmem((8, 128), f32),
            vmem((rounds + 1, 2, NZ), f32),
            vmem((rounds, 3, 2, NZ), f32),
            dma((8,)),
            dma((6, 4)),
            dma((6, 4)),
            dma((2,)),
            dma((2,)),
            dma((rounds, 3)),
            dma((rounds, 3)),
        ],
        compiler_params=pltpu.CompilerParams(
            collective_id=0, has_side_effects=True, vmem_limit_bytes=48 * 1024 * 1024
        ),
        cost_estimate=pl.CostEstimate(flops=80_000_000, bytes_accessed=4_000_000, transcendentals=0),
    )(
        in_hbm(scalars.reshape(2, CELLS, NZ)),
        in_hbm(east_wind.reshape(CELLS, NZ)),
        in_hbm(north_wind.reshape(CELLS, NZ)),
        in_hbm(up_wind.reshape(CELLS, NZ)),
        in_hbm(diffusivity.reshape(CELLS, NZ)),
        in_hbm(target_profile),
    )
    result = pl.pallas_call(
        solve,
        out_shape=jax.ShapeDtypeStruct((2, CELLS, NZ), f32),
        in_specs=[resident] * 5,
        out_specs=hbm,
        scratch_shapes=[
            vmem((2, NZ * 8, 128), f32),
            vmem((2, CELLS, NZ), f32),
            dma((2, TILES)),
        ],
        compiler_params=pltpu.CompilerParams(vmem_limit_bytes=32 * 1024 * 1024),
        cost_estimate=pl.CostEstimate(flops=2_000_000, bytes_accessed=4_000_000, transcendentals=0),
    )(*parts)
    return result.reshape(2, CX, CY, NZ)


def solution(mesh):
    placed = (
        P(None, "gx", "gy", None),
        P("gx", "gy", None),
        P("gx", "gy", None),
        P("gx", "gy", None),
        P("gx", "gy", None),
        P(),
    )
    return jax.shard_map(
        functools.partial(body, mesh.shape["gx"], mesh.shape["gy"]),
        mesh=mesh, in_specs=placed, out_specs=P(None, "gx", "gy", None), check_vma=False,
    )
```

profile of v0, /device:TPU:1, one launch (start us, length us, event | category | flops | bytes accessed | tf_op | source)
XLA Modules:
  0.0 44.0 jit_solution(11672262528426185711)
XLA Ops:
  0.0 42.0 %shard_map.64 = (f32[2,768,128]{2,1,0:T(8,128)S(1)}, f32[2,128]{1,0:T(2,128)S(1)}, f32[1152,128]{1,0:T(8,128)S(1)}, f32[1152,128]{1,0:T(8,128)S(1)}, f32[1152,128]{1,0:T(8,128)S(1)}) custom-call(f32[2,768,128]{2,1,0:T(8,128)} %bitcast.6, f32[768,128]{1,0:T(8,128)} %bitcast.7, f32[768,128]{1,0:T(8,128)} %bitcast.8, f32[768,128]{1,0:T(8,128)} %bitcast.9, ...), custom_call_target="tpu_custom_call" | custom-call | flops 80000000 | bytes 4000000 | tf_op jit(solution)/shard_map/pallas_call | solution.py:459
  42.0 2.0 %shard_map.65 = f32[2,768,128]{2,1,0:T(8,128)} custom-call(f32[2,768,128]{2,1,0:T(8,128)S(1)} %get-tuple-element.10.adv, f32[2,128]{1,0:T(2,128)S(1)} %get-tuple-element.11.shift, f32[1152,128]{1,0:T(8,128)S(1)} %get-tuple-element.12.im, f32[1152,128]{1,0:T(8,128)S(1)} %get-tuple-element.13.av, f32[1152,128]{1,0:T(8,128)S(1)} %get-tuple-element.14.cp), custom_call_target="tpu_custom_call" | custom-call | flops 2000000 | bytes 4000000 | tf_op jit(solution)/shard_map/pallas_call | solution.py:505
where the time goes:
time: 44.1 us; the launch traced here: 44 us
  Pallas kernels  44 us (100%)
    pallas_call x1, Pallas kernels, body(): pl.pallas_call(functools.partial(kernel, n_x, n_y), out_shape=[jax.ShapeD...  42 us
    pallas_call x1, Pallas kernels, body(): pl.pallas_call(solve, out_shape=jax.ShapeDtypeStruct((2, CELLS, NZ), f32)...  2.02 us

commit v1 on v0

--- a/solution.py
+++ b/solution.py
@@ -20,9 +20,10 @@
 CELLS = CX * CY
 TILES = CELLS // 128
 GROUP = 4
-ZROWS = 96
+ZROWS = 192
 PART = 24
 LEVELS = 6 * PART
+UNROLL = PART // 4
 PLACES = (0, 1, 3)
 MESH = pl.DeviceIdType.MESH
 
@@ -103,6 +104,7 @@
 
 def flux_z(u, parts, lane):
     total, g_low, g, t_low, t, t_high, r2, r1, c1, c0, l0, l1 = parts
+    u = jnp.where(lane == 0, 0.0, u)
     last = lane == NZ - 1
     t_high = jnp.where(last, -g, t_high)
     r2 = jnp.where(lane == 1, EPS2, r2)
@@ -158,23 +160,21 @@
     for peer in peers:
         pl.semaphore_signal(barrier, inc=1, device_id=peer, device_id_type=MESH)
 
-    def halo(t, way, plane=None):
+    def halo(t, way):
         st, s = lax.div(t, 2), lax.rem(t, 2)
         size = CY if way < 2 else CX
         buffer, length = (xs, CX) if way < 2 else (ys, CY)
         to = ((x_up, my), (x_dn, my), (mx, y_up), (mx, y_dn))[way]
         source, target_row = ((length, 0), (H, length + H))[way % 2]
-        first, count = (0, H) if plane is None else (plane, 1)
         return pltpu.make_async_remote_copy(
-            src_ref=buffer.at[st, s, pl.ds((source + first) * size, count * size)],
-            dst_ref=buffer.at[st, s, pl.ds((target_row + first) * size, count * size)],
+            src_ref=buffer.at[st, s, pl.ds(source * size, H * size)],
+            dst_ref=buffer.at[st, s, pl.ds(target_row * size, H * size)],
             send_sem=hsend.at[t, way], recv_sem=hrecv.at[t, way], device_id=to, device_id_type=MESH,
         )
 
     def send_halos(t, ways):
-        for plane in range(H):
-            for way in ways:
-                halo(t, way, plane).start()
+        for way in ways:
+            halo(t, way).start()
 
     def exchange(r):
         return [
@@ -212,70 +212,59 @@
     loads[0].wait()
     loads[1].wait()
     pl.semaphore_wait(barrier, len(peers))
-    for s in range(2):
+
+    def first_field(s, _):
         send_halos(s, (0, 1))
-    for s in range(2):
-
-        def convert(g, total, s=s):
-            values = [xs[0, s, pl.ds((H + g * GROUP + p) * CY, CY), :] for p in range(GROUP)]
+
+        def convert(g, total):
+            values = [xs[0, s, pl.ds(pl.multiple_of((H + g * GROUP + p) * CY, CY), CY), :] for p in range(GROUP)]
             for p, value in enumerate(values):
                 to_y(0, s, g * GROUP + p, value)
             return total + sum(values)
 
         total = lax.fori_loop(0, CX // GROUP, convert, jnp.zeros((CY, NZ), jnp.float32))
-        aro[0, s : s + 1, :] = jnp.sum(total, axis=0, keepdims=True)
+        aro[0, pl.ds(s, 1), :] = jnp.sum(total, axis=0, keepdims=True)
         send_halos(s, (2, 3))
+        return 0
+
+    lax.fori_loop(0, 2, first_field, 0)
     send_sums(0)
 
     loads[2].wait()
 
-    def scale_north(g, _):
-        values = [nraw[pl.ds((g * GROUP + p) * CY, CY), :] * (1.0 / 6.0) for p in range(GROUP)]
+    def turn_north(g, _):
+        values = [nraw[pl.ds(pl.multiple_of((g * GROUP + p) * CY, CY), CY), :] for p in range(GROUP)]
         for p, value in enumerate(values):
             for i in range(CY // 8):
                 ny[pl.ds(8 * i * CX + g * GROUP + p, 8, stride=CX), :] = value[8 * i : 8 * i + 8]
         return 0
 
-    lax.fori_loop(0, CX // GROUP, scale_north, 0)
+    lax.fori_loop(0, CX // GROUP, turn_north, 0)
     north_edge.start()
     loads[3].wait()
 
-    def scale_east(g, _):
-        rows = pl.ds(pl.multiple_of(g * GROUP * CY, CY), GROUP * CY)
-        ex[rows, :] = ex[rows, :] * (1.0 / 6.0)
-        return 0
-
-    lax.fori_loop(0, CX // GROUP, scale_east, 0)
     east_edge.start()
     loads[5].wait()
     lane = lax.broadcasted_iota(jnp.int32, (8, NZ), 1)
-    lane_all = lax.broadcasted_iota(jnp.int32, (GROUP * CY, NZ), 1)
-
-    def scale_up(g, _):
-        rows = pl.ds(pl.multiple_of(g * GROUP * CY, CY), GROUP * CY)
-        uz[rows, :] = jnp.where(lane_all == 0, 0.0, uz[rows, :] * (1.0 / 6.0))
-        return 0
-
-    lax.fori_loop(0, CX // GROUP, scale_up, 0)
 
     loads[4].wait()
     loads[6].wait()
     loads[7].wait()
-    for c in range(8):
-        if c < TILES:
-            levels = jnp.transpose(kd[pl.ds(c * 128, 128), :]) * STEP
-        else:
-            levels = jnp.zeros((NZ, 128), jnp.float32)
-        fk[pl.ds(c, NZ, stride=8), :] = levels
+
+    def columns_to_lanes(c, _):
+        rows = pl.ds(pl.multiple_of(c * 128, 128), 128)
+        fk[pl.ds(c, NZ, stride=8), :] = jnp.transpose(kd[rows, :]) * STEP
+        return 0
+
+    fk[...] = jnp.zeros(fk.shape, jnp.float32)
+    lax.fori_loop(0, TILES, columns_to_lanes, 0)
     fk[pl.ds(0, 8), :] = jnp.zeros((8, 128), jnp.float32)
-    fk[pl.ds(NZ * 8, (LEVELS - NZ + 1) * 8), :] = jnp.zeros(((LEVELS - NZ + 1) * 8, 128), jnp.float32)
     es[...] = jnp.zeros((8, 128), jnp.float32)
 
-    def factor(part):
-        base = pl.multiple_of(part * (PART * 8), 8)
+    def factor(first, e):
+        base = pl.multiple_of(first * 8, 8)
         low = fk[pl.ds(base, 8), :]
-        e = es[...]
-        for i in range(PART):
+        for i in range(UNROLL):
             row = pl.ds(base + 8 * i, 8)
             above = fk[pl.ds(base + 8 * i + 8, 8), :]
             g = 1.0 + low * e
@@ -285,7 +274,7 @@
             av[row, :] = low * inverse
             cp[row, :] = above * inverse
             low = above
-        es[...] = e
+        return e
 
     def x_faces(st, s, row, first, last):
         flux = march(
@@ -305,39 +294,27 @@
         for y in range(first, last):
             ty[pl.ds(row * CY + y, 8, stride=CY), :] = flux[y - first] - flux[y - first + 1]
 
-    def z_faces(st, s):
-        groups = CELLS // ZROWS
-
-        def group(i, _):
-            late = pl.multiple_of(lax.max(i - 1, 0) * ZROWS, ZROWS)
-            now = pl.multiple_of(lax.min(i, groups - 1) * ZROWS, ZROWS)
-            for v in range(ZROWS // 8):
-                flux = flux_z(
-                    uz[pl.ds(late + 8 * v, 8), :], [zs[part, 8 * v : 8 * v + 8, :] for part in range(12)], lane
-                )
-                fz[pl.ds(late + 8 * v, 8), :] = flux
-                fr[pl.ds(late + 8 * v, 8), :] = pltpu.roll(flux, NZ - 1, 1)
-            for v in range(ZROWS // 8):
-                parts = shifted_z(xs[st, s, pl.ds(H * CY + now + 8 * v, 8), :], lane)
-                for part in range(12):
-                    zs[part, 8 * v : 8 * v + 8, :] = parts[part]
-            return 0
-
-        lax.fori_loop(0, groups + 1, group, 0)
-
-    def columns(count, work):
-        def block(i, _):
-            work(pl.multiple_of(i * 8, 8))
-            return 0
-
-        lax.fori_loop(0, count, block, 0)
+    def z_faces(st, s, first):
+        for v in range(ZROWS // 8):
+            parts = shifted_z(xs[st, s, pl.ds(H * CY + first + 8 * v, 8), :], lane)
+            for part in range(12):
+                zs[part, 8 * v : 8 * v + 8, :] = parts[part]
+        for v in range(ZROWS // 8):
+            rows = pl.ds(first + 8 * v, 8)
+            flux = flux_z(uz[rows, :], [zs[part, 8 * v : 8 * v + 8, :] for part in range(12)], lane)
+            fz[rows, :] = flux
+            fr[rows, :] = pltpu.roll(flux, NZ - 1, 1)
 
     def step(t, _):
         st, s = lax.div(t, 2), lax.rem(t, 2)
-        factor(t)
-        columns(CX // 8, lambda row: y_faces(st, s, row, H, CY - H))
-        columns(CY // 8, lambda row: x_faces(st, s, row, H, CX - H))
-        z_faces(st, s)
+
+        def interior(i, e):
+            y_faces(st, s, pl.multiple_of(lax.min(i, CX // 8 - 1) * 8, 8), H, CY - H)
+            x_faces(st, s, pl.multiple_of(i * 8, 8), H, CX - H)
+            z_faces(st, s, pl.multiple_of(i * ZROWS, 8))
+            return factor(t * PART + i * UNROLL, e)
+
+        es[...] = lax.fori_loop(0, CELLS // ZROWS, interior, es[...])
         for r, place in enumerate(PLACES[: rounds - 1]):
 
             @pl.when(t == place)
@@ -351,20 +328,36 @@
             north_edge.wait_recv()
             east_edge.wait_recv()
 
-        halo(t, 2).wait_recv()
-        halo(t, 3).wait_recv()
-        columns(CX // 8, lambda row: (y_faces(st, s, row, 0, H), y_faces(st, s, row, CY - H, CY)))
-        halo(t, 0).wait_recv()
-        halo(t, 1).wait_recv()
-        columns(CY // 8, lambda row: (x_faces(st, s, row, 0, H), x_faces(st, s, row, CX - H, CX)))
-        coef = jnp.where(st == 0, STEP / 3.0, jnp.where(st == 1, STEP * 0.5, STEP)).astype(jnp.float32)
+        for way in range(4):
+            halo(t, way).wait_recv()
+
+        def boundary(i, _):
+            for k in range(2):
+                row = pl.multiple_of(i * 16 + 8 * k, 8)
+                x_faces(st, s, row, 0, H)
+                x_faces(st, s, row, CX - H, CX)
+                row = pl.multiple_of(lax.min(2 * i + k, CX // 8 - 1) * 8, 8)
+                y_faces(st, s, row, 0, H)
+                y_faces(st, s, row, CY - H, CY)
+            return 0
+
+        lax.fori_loop(0, CY // 16, boundary, 0)
+        coef = jnp.where(st == 0, STEP / 18.0, jnp.where(st == 1, STEP / 12.0, STEP / 6.0)).astype(jnp.float32)
 
         def update(g, _):
             rows = pl.ds(pl.multiple_of(g * GROUP * CY, CY), GROUP * CY)
             value = bs[s, rows, :] + coef * (tx[rows, :] + ty[rows, :] + (fz[rows, :] - fr[rows, :]))
-            xs[st + 1, s, pl.ds(pl.multiple_of((H + g * GROUP) * CY, CY), GROUP * CY), :] = value
-            for p in range(GROUP):
-                to_y(st + 1, s, g * GROUP + p, value[p * CY : (p + 1) * CY])
+
+            @pl.when(st < 2)
+            def _():
+                xs[st + 1, s, pl.ds(pl.multiple_of((H + g * GROUP) * CY, CY), GROUP * CY), :] = value
+                for p in range(GROUP):
+                    to_y(st + 1, s, g * GROUP + p, value[p * CY : (p + 1) * CY])
+
+            @pl.when(st == 2)
+            def _():
+                adv[s, rows, :] = value
+
             return 0
 
         lax.fori_loop(0, CX // GROUP, update, 0)
@@ -380,8 +373,6 @@
     add_sums(rounds - 1)
     cells = float(n_x * CX * n_y * CY)
     shift[...] = RELAX * (aro[rounds] * (1.0 / cells) - tg[...])
-    for s in range(2):
-        adv[s] = xs[3, s, pl.ds(H * CY, CELLS), :]
 
     def drain(t, _):
         for way in range(4):
@@ -464,9 +455,9 @@
         in_specs=[hbm] * 6,
         out_specs=[resident] * 5,
         scratch_shapes=[
-            vmem((4, 2, XROWS, NZ), f32),
+            vmem((3, 2, XROWS, NZ), f32),
             vmem((2, CELLS, NZ), f32),
-            vmem((4, 2, YROWS, NZ), f32),
+            vmem((3, 2, YROWS, NZ), f32),
             vmem((12, ZROWS, NZ), f32),
             vmem((CELLS, NZ), f32),
             vmem((CELLS, NZ), f32),

time: 44.1 us -> 46.9 us (1.063)
  Pallas kernels: 44 us -> 46.8 us
    pallas_call x1, Pallas kernels: 42 us -> 44.8 us  [body(): pl.pallas_call(functools.partial(kernel, n_x, n_y), out_shape=[jax.ShapeD...]
where the time goes in v1:
time: 46.9 us; the launch traced here: 46.8 us
  Pallas kernels  46.8 us (100%)
    pallas_call x1, Pallas kernels, body(): pl.pallas_call(functools.partial(kernel, n_x, n_y), out_shape=[jax.ShapeD...  44.8 us
    pallas_call x1, Pallas kernels, body(): pl.pallas_call(solve, out_shape=jax.ShapeDtypeStruct((2, CELLS, NZ), f32)...  2.02 us

profile of v1, /device:TPU:1, one launch (start us, length us, event | category | flops | bytes accessed | tf_op | source)
XLA Modules:
  0.0 46.8 jit_solution(5173164521718899612)
XLA Ops:
  0.0 44.8 %shard_map.64 = (f32[2,768,128]{2,1,0:T(8,128)S(1)}, f32[2,128]{1,0:T(2,128)S(1)}, f32[1152,128]{1,0:T(8,128)S(1)}, f32[1152,128]{1,0:T(8,128)S(1)}, f32[1152,128]{1,0:T(8,128)S(1)}) custom-call(f32[2,768,128]{2,1,0:T(8,128)} %bitcast.6, f32[768,128]{1,0:T(8,128)} %bitcast.7, f32[768,128]{1,0:T(8,128)} %bitcast.8, f32[768,128]{1,0:T(8,128)} %bitcast.9, ...), custom_call_target="tpu_custom_call" | custom-call | flops 80000000 | bytes 4000000 | tf_op jit(solution)/shard_map/pallas_call | solution.py:450
  44.8 2.0 %shard_map.65 = f32[2,768,128]{2,1,0:T(8,128)} custom-call(f32[2,768,128]{2,1,0:T(8,128)S(1)} %get-tuple-element.10.adv, f32[2,128]{1,0:T(2,128)S(1)} %get-tuple-element.11.shift, f32[1152,128]{1,0:T(8,128)S(1)} %get-tuple-element.12.im, f32[1152,128]{1,0:T(8,128)S(1)} %get-tuple-element.13.av, f32[1152,128]{1,0:T(8,128)S(1)} %get-tuple-element.14.cp), custom_call_target="tpu_custom_call" | custom-call | flops 2000000 | bytes 4000000 | tf_op jit(solution)/shard_map/pallas_call | solution.py:496

commit v2 on v1

--- a/solution.py
+++ b/solution.py
@@ -19,7 +19,7 @@
 YROWS = (CY + 2 * H) * CX
 CELLS = CX * CY
 TILES = CELLS // 128
-GROUP = 4
+GROUP = 8
 ZROWS = 192
 PART = 24
 LEVELS = 6 * PART
@@ -88,28 +88,45 @@
     return out
 
 
+def joined(flux, part, edge, row):
+    rows = pl.ds(row, 8)
+    if part == 0:
+        return flux + [edge[0, rows, :]]
+    if part == 2:
+        return [edge[1, rows, :]] + flux
+    edge[0, rows, :] = flux[0]
+    edge[1, rows, :] = flux[-1]
+    return flux
+
+
 def shifted_z(f, lane):
-    below, below2, above = pltpu.roll(f, 1, 1), pltpu.roll(f, 2, 1), pltpu.roll(f, NZ - 1, 1)
+    below = pltpu.roll(f, 1, 1)
     d = jnp.where(lane == 0, 0.0, f - below)
-    d_low = jnp.where(lane <= 1, 0.0, below - below2)
-    d_high = jnp.where(lane == NZ - 1, 0.0, above - f)
-    g, left, mid, right = cell(d, 0.75 * d, d_high, 0.75 * d_high)
-    g_low = d - d_low
-    t = g - g_low
     return (
-        f + below, g_low, g, pltpu.roll(t, 1, 1), t, pltpu.roll(t, NZ - 1, 1), pltpu.roll(right, 2, 1),
-        pltpu.roll(right, 1, 1), pltpu.roll(mid, 1, 1), mid, left, pltpu.roll(left, NZ - 1, 1),
+        f + below, d, jnp.where(lane == 1, 0.0, pltpu.roll(d, 2, 1)), pltpu.roll(d, 1, 1), pltpu.roll(d, NZ - 1, 1),
+        jnp.where(lane == NZ - 1, 0.0, pltpu.roll(d, NZ - 2, 1)),
     )
 
 
 def flux_z(u, parts, lane):
-    total, g_low, g, t_low, t, t_high, r2, r1, c1, c0, l0, l1 = parts
+    total, d3, low2, low1, high1, high2 = parts
     u = jnp.where(lane == 0, 0.0, u)
-    last = lane == NZ - 1
-    t_high = jnp.where(last, -g, t_high)
-    r2 = jnp.where(lane == 1, EPS2, r2)
-    l1 = jnp.where(last, EPS2, l1)
-    return face(u, total, g_low, g, t_low, t, t_high, r2, r1, c1, c0, l0, l1)
+    pos = u > 0.0
+    d1 = jnp.where(pos, low2, high2)
+    d2 = jnp.where(pos, low1, high1)
+    d4 = jnp.where(pos, high1, low1)
+    g0, g1, g2 = d2 - d1, d3 - d2, d4 - d3
+    e2, e3 = 0.75 * d2, 0.75 * d3
+    b0 = (g0 * g0 + EPS) + e2 * (d2 + g0)
+    b1 = (g1 * g1 + EPS) + e3 * d2
+    b2 = (g2 * g2 + EPS) + e3 * (d3 - g2)
+    b0 = 3.0 * (b0 * b0)
+    b1 = b1 * b1
+    b2 = b2 * b2
+    c2 = b2 + b2
+    num = b1 * (c2 * (g1 - g0) + b0 * (g2 - g1))
+    den = b1 * (b2 + b0) + b0 * c2
+    return u * (3.0 * total) - jnp.abs(u) * (g1 + num * pl.reciprocal(den, approx=True))
 
 
 def digits(n):
@@ -124,7 +141,7 @@
 def kernel(
     n_x, n_y,
     scal, east, north, upw, diff, target, adv, shift, im, av, cp,
-    xs, bs, ys, zs, fz, fr, tx, ty, ex, ny, nraw, uz, kd, tg, fk, es, aro, ari,
+    xs, bs, ys, edge, tz, tx, ty, ex, ny, nraw, uz, kd, tg, fk, es, aro, ari,
     lsem, hsend, hrecv, wsend, wrecv, asend, arecv,
 ):
     mx, my = lax.axis_index("gx"), lax.axis_index("gy")
@@ -276,45 +293,55 @@
             low = above
         return e
 
-    def x_faces(st, s, row, first, last):
+    def x_faces(st, s, row, part):
+        first, last = ((0, H), (H, CX - H), (CX - H, CX))[part]
         flux = march(
             lambda x: xs[st, s, pl.ds((H + x) * CY + row, 8), :],
             lambda x: ex[pl.ds(x * CY + row, 8), :],
-            first, last,
+            first + (part == 2), last - (part == 0),
         )
+        flux = joined(flux, part, edge, row)
         for x in range(first, last):
             tx[pl.ds(x * CY + row, 8), :] = flux[x - first] - flux[x - first + 1]
 
-    def y_faces(st, s, row, first, last):
+    def y_faces(st, s, row, part):
+        first, last = ((0, H), (H, CY - H), (CY - H, CY))[part]
         flux = march(
             lambda y: ys[st, s, pl.ds((H + y) * CX + row, 8), :],
             lambda y: ny[pl.ds(y * CX + row, 8), :],
-            first, last,
+            first + (part == 2), last - (part == 0),
         )
+        flux = joined(flux, part, edge, CY + row)
         for y in range(first, last):
             ty[pl.ds(row * CY + y, 8, stride=CY), :] = flux[y - first] - flux[y - first + 1]
 
-    def z_faces(st, s, first):
-        for v in range(ZROWS // 8):
-            parts = shifted_z(xs[st, s, pl.ds(H * CY + first + 8 * v, 8), :], lane)
-            for part in range(12):
-                zs[part, 8 * v : 8 * v + 8, :] = parts[part]
-        for v in range(ZROWS // 8):
-            rows = pl.ds(first + 8 * v, 8)
-            flux = flux_z(uz[rows, :], [zs[part, 8 * v : 8 * v + 8, :] for part in range(12)], lane)
-            fz[rows, :] = flux
-            fr[rows, :] = pltpu.roll(flux, NZ - 1, 1)
+    def z_faces(st, s):
+        def group(i, _):
+            first = pl.multiple_of(i * ZROWS, ZROWS)
+            rows = [pl.ds(first + 8 * v, 8) for v in range(ZROWS // 8)]
+            parts = [shifted_z(xs[st, s, pl.ds(H * CY + first + 8 * v, 8), :], lane) for v in range(ZROWS // 8)]
+            flux = [flux_z(uz[r, :], part, lane) for r, part in zip(rows, parts)]
+            for r, value in zip(rows, flux):
+                tz[r, :] = value - pltpu.roll(value, NZ - 1, 1)
+            return 0
+
+        lax.fori_loop(0, CELLS // ZROWS, group, 0)
 
     def step(t, _):
         st, s = lax.div(t, 2), lax.rem(t, 2)
 
-        def interior(i, e):
-            y_faces(st, s, pl.multiple_of(lax.min(i, CX // 8 - 1) * 8, 8), H, CY - H)
-            x_faces(st, s, pl.multiple_of(i * 8, 8), H, CX - H)
-            z_faces(st, s, pl.multiple_of(i * ZROWS, 8))
+        def y_inner(i, _):
+            y_faces(st, s, pl.multiple_of(i * 8, 8), 1)
+            return 0
+
+        lax.fori_loop(0, CX // 8, y_inner, 0)
+
+        def x_inner(i, e):
+            x_faces(st, s, pl.multiple_of(i * 8, 8), 1)
             return factor(t * PART + i * UNROLL, e)
 
-        es[...] = lax.fori_loop(0, CELLS // ZROWS, interior, es[...])
+        es[...] = lax.fori_loop(0, CY // 8, x_inner, es[...])
+        z_faces(st, s)
         for r, place in enumerate(PLACES[: rounds - 1]):
 
             @pl.when(t == place)
@@ -328,25 +355,26 @@
             north_edge.wait_recv()
             east_edge.wait_recv()
 
-        for way in range(4):
-            halo(t, way).wait_recv()
-
-        def boundary(i, _):
+        halo(t, 2).wait_recv()
+        halo(t, 3).wait_recv()
+        for row in range(0, CX, 8):
+            y_faces(st, s, row, 0)
+            y_faces(st, s, row, 2)
+        halo(t, 0).wait_recv()
+        halo(t, 1).wait_recv()
+
+        def x_outer(i, _):
             for k in range(2):
-                row = pl.multiple_of(i * 16 + 8 * k, 8)
-                x_faces(st, s, row, 0, H)
-                x_faces(st, s, row, CX - H, CX)
-                row = pl.multiple_of(lax.min(2 * i + k, CX // 8 - 1) * 8, 8)
-                y_faces(st, s, row, 0, H)
-                y_faces(st, s, row, CY - H, CY)
+                x_faces(st, s, pl.multiple_of(i * 16 + 8 * k, 8), 0)
+                x_faces(st, s, pl.multiple_of(i * 16 + 8 * k, 8), 2)
             return 0
 
-        lax.fori_loop(0, CY // 16, boundary, 0)
+        lax.fori_loop(0, CY // 16, x_outer, 0)
         coef = jnp.where(st == 0, STEP / 18.0, jnp.where(st == 1, STEP / 12.0, STEP / 6.0)).astype(jnp.float32)
 
         def update(g, _):
             rows = pl.ds(pl.multiple_of(g * GROUP * CY, CY), GROUP * CY)
-            value = bs[s, rows, :] + coef * (tx[rows, :] + ty[rows, :] + (fz[rows, :] - fr[rows, :]))
+            value = bs[s, rows, :] + coef * (tx[rows, :] + ty[rows, :] + tz[rows, :])
 
             @pl.when(st < 2)
             def _():
@@ -458,8 +486,7 @@
             vmem((3, 2, XROWS, NZ), f32),
             vmem((2, CELLS, NZ), f32),
             vmem((3, 2, YROWS, NZ), f32),
-            vmem((12, ZROWS, NZ), f32),
-            vmem((CELLS, NZ), f32),
+            vmem((2, CY + CX, NZ), f32),
             vmem((CELLS, NZ), f32),
             vmem((CELLS, NZ), f32),
             vmem((CELLS, NZ), f32),

time: 46.9 us -> 37.6 us (0.80)
  Pallas kernels: 46.8 us -> 37.5 us
    pallas_call x1, Pallas kernels: 44.8 us -> 35.5 us  [body(): pl.pallas_call(functools.partial(kernel, n_x, n_y), out_shape=[jax.ShapeD...]
where the time goes in v2:
time: 37.6 us; the launch traced here: 37.5 us
  Pallas kernels  37.5 us (100%)
    pallas_call x1, Pallas kernels, body(): pl.pallas_call(functools.partial(kernel, n_x, n_y), out_shape=[jax.ShapeD...  35.5 us
    pallas_call x1, Pallas kernels, body(): pl.pallas_call(solve, out_shape=jax.ShapeDtypeStruct((2, CELLS, NZ), f32)...  2.02 us

profile of v2, /device:TPU:1, one launch (start us, length us, event | category | flops | bytes accessed | tf_op | source)
XLA Modules:
  0.0 37.5 jit_solution(2193146314221856063)
XLA Ops:
  0.0 35.5 %shard_map.64 = (f32[2,768,128]{2,1,0:T(8,128)S(1)}, f32[2,128]{1,0:T(2,128)S(1)}, f32[1152,128]{1,0:T(8,128)S(1)}, f32[1152,128]{1,0:T(8,128)S(1)}, f32[1152,128]{1,0:T(8,128)S(1)}) custom-call(f32[2,768,128]{2,1,0:T(8,128)} %bitcast.6, f32[768,128]{1,0:T(8,128)} %bitcast.7, f32[768,128]{1,0:T(8,128)} %bitcast.8, f32[768,128]{1,0:T(8,128)} %bitcast.9, ...), custom_call_target="tpu_custom_call" | custom-call | flops 80000000 | bytes 4000000 | tf_op jit(solution)/shard_map/pallas_call | solution.py:478
  35.5 2.0 %shard_map.65 = f32[2,768,128]{2,1,0:T(8,128)} custom-call(f32[2,768,128]{2,1,0:T(8,128)S(1)} %get-tuple-element.10.adv, f32[2,128]{1,0:T(2,128)S(1)} %get-tuple-element.11.shift, f32[1152,128]{1,0:T(8,128)S(1)} %get-tuple-element.12.im, f32[1152,128]{1,0:T(8,128)S(1)} %get-tuple-element.13.av, f32[1152,128]{1,0:T(8,128)S(1)} %get-tuple-element.14.cp), custom_call_target="tpu_custom_call" | custom-call | flops 2000000 | bytes 4000000 | tf_op jit(solution)/shard_map/pallas_call | solution.py:523

commit v3 on v2

--- a/solution.py
+++ b/solution.py
@@ -15,6 +15,7 @@
 
 CX, CY, NZ = 24, 32, 128
 H = 3
+HALF = H * 32 // 2
 XROWS = (CX + 2 * H) * CY
 YROWS = (CY + 2 * H) * CX
 CELLS = CX * CY
@@ -24,7 +25,7 @@
 PART = 24
 LEVELS = 6 * PART
 UNROLL = PART // 4
-PLACES = (0, 1, 3)
+PLACES = (0, 2, 4)
 MESH = pl.DeviceIdType.MESH
 
 
@@ -141,14 +142,23 @@
 def kernel(
     n_x, n_y,
     scal, east, north, upw, diff, target, adv, shift, im, av, cp,
-    xs, bs, ys, edge, tz, tx, ty, ex, ny, nraw, uz, kd, tg, fk, es, aro, ari,
-    lsem, hsend, hrecv, wsend, wrecv, asend, arecv,
+    xs, bs, ys, edge, tz, tx, ty, ex, ny, nraw, uz, kd, tg, fk, es, aro, ari, held,
+    lsem, hsend, hrecv, nsend, nrecv, fsend, frecv, gsend, grecv, wsend, wrecv, asend, arecv,
 ):
     mx, my = lax.axis_index("gx"), lax.axis_index("gy")
     x_up, x_dn = lax.rem(mx + 1, n_x), lax.rem(mx + n_x - 1, n_x)
     y_up, y_dn = lax.rem(my + 1, n_y), lax.rem(my + n_y - 1, n_y)
     plan = [("x", d) for d in digits(n_x)] + [("y", d) for d in digits(n_y)]
     rounds = len(plan)
+    core = lax.rem(mx, 2)
+    my_side = my + 1 - 2 * lax.rem(my, 2)
+    flip = mx + 2 - 4 * lax.rem(lax.div(mx, 2), 2)
+
+    def far(index):
+        return lax.rem(index + 2 * core - 1 + n_x, n_x)
+
+    near, beyond = mx + 1 - 2 * core, far(mx)
+    flip_back = beyond + 2 - 4 * lax.rem(lax.div(beyond, 2), 2)
 
     def partner(r, k):
         axis, (stride, radix) = plan[r]
@@ -171,27 +181,57 @@
         load.start()
 
     barrier = pltpu.get_barrier_semaphore()
-    peers = [(x_up, my), (x_dn, my), (mx, y_up), (mx, y_dn)] + [
-        partner(r, k) for r in range(rounds) for k in range(1, plan[r][1][1])
-    ]
-    for peer in peers:
-        pl.semaphore_signal(barrier, inc=1, device_id=peer, device_id_type=MESH)
-
-    def halo(t, way):
+    sums = [partner(r, k) for r in range(rounds) for k in range(1, plan[r][1][1])]
+    both = [(near, my), (mx, my_side), (flip, my_side), (beyond, my_side), (mx, y_up), (mx, y_dn)] + sums
+    sources = both + [(x_up, my), (flip_back, my_side)]
+    targets = both + [(x_dn, my), (far(flip), my_side)]
+    for source in sources:
+        pl.semaphore_signal(barrier, inc=1, device_id=source, device_id_type=MESH)
+
+    def remote(src, dst, send, recv, to):
+        return pltpu.make_async_remote_copy(
+            src_ref=src, dst_ref=dst, send_sem=send, recv_sem=recv, device_id=to, device_id_type=MESH
+        )
+
+    def x_rows(t, plane, first, count):
+        row = pl.multiple_of(plane * CY + first, 8)
+        return xs.at[lax.div(t, 2), lax.rem(t, 2), pl.ds(row, count)]
+
+    def x_near(t):
+        src = x_rows(t, H + (1 - core) * (CX - H), 0, H * CY)
+        return remote(src, x_rows(t, core * (CX + H), 0, H * CY), nsend.at[t], nrecv.at[t], (near, my))
+
+    def x_first(t, half):
+        src = x_rows(t, H + core * (CX - H), half * HALF, HALF)
+        to = ((mx, my_side), (flip, my_side))[half]
+        return remote(src, held.at[t, half], fsend.at[t, half], frecv.at[t, half], to)
+
+    def x_second(t, half):
+        dst = x_rows(t, (1 - core) * (CX + H), half * HALF, HALF)
+        to = ((beyond, my_side), (far(flip), my_side))[half]
+        return remote(held.at[t, half], dst, gsend.at[t, half], grecv.at[t, half], to)
+
+    def y_halo(t, way):
         st, s = lax.div(t, 2), lax.rem(t, 2)
-        size = CY if way < 2 else CX
-        buffer, length = (xs, CX) if way < 2 else (ys, CY)
-        to = ((x_up, my), (x_dn, my), (mx, y_up), (mx, y_dn))[way]
-        source, target_row = ((length, 0), (H, length + H))[way % 2]
-        return pltpu.make_async_remote_copy(
-            src_ref=buffer.at[st, s, pl.ds(source * size, H * size)],
-            dst_ref=buffer.at[st, s, pl.ds(target_row * size, H * size)],
-            send_sem=hsend.at[t, way], recv_sem=hrecv.at[t, way], device_id=to, device_id_type=MESH,
+        source, target_row = ((CY, 0), (H, CY + H))[way]
+        return remote(
+            ys.at[st, s, pl.ds(source * CX, H * CX)], ys.at[st, s, pl.ds(target_row * CX, H * CX)],
+            hsend.at[t, way], hrecv.at[t, way], (mx, (y_up, y_dn)[way]),
         )
 
-    def send_halos(t, ways):
-        for way in ways:
-            halo(t, way).start()
+    def send_x(t):
+        x_first(t, 0).start()
+        x_first(t, 1).start()
+        x_near(t).start()
+
+    def send_y(t):
+        y_halo(t, 0).start()
+        y_halo(t, 1).start()
+
+    def forward(t):
+        for half in range(2):
+            x_first(t, half).wait_recv()
+            x_second(t, half).start()
 
     def exchange(r):
         return [
@@ -228,10 +268,10 @@
 
     loads[0].wait()
     loads[1].wait()
-    pl.semaphore_wait(barrier, len(peers))
+    pl.semaphore_wait(barrier, len(targets))
 
     def first_field(s, _):
-        send_halos(s, (0, 1))
+        send_x(s)
 
         def convert(g, total):
             values = [xs[0, s, pl.ds(pl.multiple_of((H + g * GROUP + p) * CY, CY), CY), :] for p in range(GROUP)]
@@ -241,7 +281,7 @@
 
         total = lax.fori_loop(0, CX // GROUP, convert, jnp.zeros((CY, NZ), jnp.float32))
         aro[0, pl.ds(s, 1), :] = jnp.sum(total, axis=0, keepdims=True)
-        send_halos(s, (2, 3))
+        send_y(s)
         return 0
 
     lax.fori_loop(0, 2, first_field, 0)
@@ -327,6 +367,8 @@
 
         lax.fori_loop(0, CELLS // ZROWS, group, 0)
 
+    forward(0)
+
     def step(t, _):
         st, s = lax.div(t, 2), lax.rem(t, 2)
 
@@ -342,6 +384,10 @@
 
         es[...] = lax.fori_loop(0, CY // 8, x_inner, es[...])
         z_faces(st, s)
+        @pl.when(t < 5)
+        def _():
+            forward(t + 1)
+
         for r, place in enumerate(PLACES[: rounds - 1]):
 
             @pl.when(t == place)
@@ -355,13 +401,14 @@
             north_edge.wait_recv()
             east_edge.wait_recv()
 
-        halo(t, 2).wait_recv()
-        halo(t, 3).wait_recv()
+        y_halo(t, 0).wait_recv()
+        y_halo(t, 1).wait_recv()
         for row in range(0, CX, 8):
             y_faces(st, s, row, 0)
             y_faces(st, s, row, 2)
-        halo(t, 0).wait_recv()
-        halo(t, 1).wait_recv()
+        x_near(t).wait_recv()
+        x_second(t, 0).wait_recv()
+        x_second(t, 1).wait_recv()
 
         def x_outer(i, _):
             for k in range(2):
@@ -392,7 +439,8 @@
 
         @pl.when(st < 2)
         def _():
-            send_halos(t + 2, range(4))
+            send_x(t + 2)
+            send_y(t + 2)
 
         return 0
 
@@ -403,8 +451,11 @@
     shift[...] = RELAX * (aro[rounds] * (1.0 / cells) - tg[...])
 
     def drain(t, _):
-        for way in range(4):
-            halo(t, way).wait_send()
+        x_near(t).wait_send()
+        for k in range(2):
+            x_first(t, k).wait_send()
+            x_second(t, k).wait_send()
+            y_halo(t, k).wait_send()
         return 0
 
     lax.fori_loop(0, 6, drain, 0)
@@ -500,9 +551,16 @@
             vmem((8, 128), f32),
             vmem((rounds + 1, 2, NZ), f32),
             vmem((rounds, 3, 2, NZ), f32),
+            vmem((6, 2, HALF, NZ), f32),
             dma((8,)),
-            dma((6, 4)),
-            dma((6, 4)),
+            dma((6, 2)),
+            dma((6, 2)),
+            dma((6,)),
+            dma((6,)),
+            dma((6, 2)),
+            dma((6, 2)),
+            dma((6, 2)),
+            dma((6, 2)),
             dma((2,)),
             dma((2,)),
             dma((rounds, 3)),

time: 37.6 us -> 40.2 us (1.069)
  Pallas kernels: 37.5 us -> 40.1 us
    pallas_call x1, Pallas kernels: 35.5 us -> 38.1 us  [body(): pl.pallas_call(functools.partial(kernel, n_x, n_y), out_shape=[jax.ShapeD...]
where the time goes in v3:
time: 40.2 us; the launch traced here: 40.1 us
  Pallas kernels  40.1 us (100%)
    pallas_call x1, Pallas kernels, body(): pl.pallas_call(functools.partial(kernel, n_x, n_y), out_shape=[jax.ShapeD...  38.1 us
    pallas_call x1, Pallas kernels, body(): pl.pallas_call(solve, out_shape=jax.ShapeDtypeStruct((2, CELLS, NZ), f32)...  2.02 us

profile of v3, /device:TPU:1, one launch (start us, length us, event | category | flops | bytes accessed | tf_op | source)
XLA Modules:
  0.0 40.1 jit_solution(13725080312983253463)
XLA Ops:
  0.0 38.1 %shard_map.64 = (f32[2,768,128]{2,1,0:T(8,128)S(1)}, f32[2,128]{1,0:T(2,128)S(1)}, f32[1152,128]{1,0:T(8,128)S(1)}, f32[1152,128]{1,0:T(8,128)S(1)}, f32[1152,128]{1,0:T(8,128)S(1)}) custom-call(f32[2,768,128]{2,1,0:T(8,128)} %bitcast.6, f32[768,128]{1,0:T(8,128)} %bitcast.7, f32[768,128]{1,0:T(8,128)} %bitcast.8, f32[768,128]{1,0:T(8,128)} %bitcast.9, ...), custom_call_target="tpu_custom_call" | custom-call | flops 80000000 | bytes 4000000 | tf_op jit(solution)/shard_map/pallas_call | solution.py:529
  38.1 2.0 %shard_map.65 = f32[2,768,128]{2,1,0:T(8,128)} custom-call(f32[2,768,128]{2,1,0:T(8,128)S(1)} %get-tuple-element.10.adv, f32[2,128]{1,0:T(2,128)S(1)} %get-tuple-element.11.shift, f32[1152,128]{1,0:T(8,128)S(1)} %get-tuple-element.12.im, f32[1152,128]{1,0:T(8,128)S(1)} %get-tuple-element.13.av, f32[1152,128]{1,0:T(8,128)S(1)} %get-tuple-element.14.cp), custom_call_target="tpu_custom_call" | custom-call | flops 2000000 | bytes 4000000 | tf_op jit(solution)/shard_map/pallas_call | solution.py:581

commit v4 on v2

--- a/solution.py
+++ b/solution.py
@@ -21,10 +21,9 @@
 TILES = CELLS // 128
 GROUP = 8
 ZROWS = 192
-PART = 24
-LEVELS = 6 * PART
-UNROLL = PART // 4
-PLACES = (0, 1, 3)
+PART = 48
+LEVELS = 3 * PART
+UNROLL = PART // 8
 MESH = pl.DeviceIdType.MESH
 
 
@@ -130,12 +129,10 @@
 
 
 def digits(n):
-    out, stride = [], 1
-    while stride < n:
-        radix = min(4, n // stride)
-        out.append((stride, radix))
-        stride *= radix
-    return out
+    radix, count = min(4, n), 1
+    while radix**count < n:
+        count += 1
+    return count, radix
 
 
 def kernel(
@@ -147,15 +144,15 @@
     mx, my = lax.axis_index("gx"), lax.axis_index("gy")
     x_up, x_dn = lax.rem(mx + 1, n_x), lax.rem(mx + n_x - 1, n_x)
     y_up, y_dn = lax.rem(my + 1, n_y), lax.rem(my + n_y - 1, n_y)
-    plan = [("x", d) for d in digits(n_x)] + [("y", d) for d in digits(n_y)]
-    rounds = len(plan)
+    per_axis, radix = digits(n_x)
+    rounds = 2 * per_axis
 
     def partner(r, k):
-        axis, (stride, radix) = plan[r]
-        me = mx if axis == "x" else my
+        on_x, stride = 1 - r // per_axis, 1 + (r % per_axis) * (radix - 1)
+        me = on_x * mx + (1 - on_x) * my
         digit = lax.rem(lax.div(me, stride), radix)
         other = me + stride * (lax.rem(digit + k, radix) - digit)
-        return (other, my) if axis == "x" else (mx, other)
+        return on_x * other + (1 - on_x) * mx, on_x * my + (1 - on_x) * other
 
     loads = [
         pltpu.make_async_copy(scal.at[0], xs.at[0, 0, pl.ds(H * CY, CELLS)], lsem.at[0]),
@@ -172,7 +169,7 @@
 
     barrier = pltpu.get_barrier_semaphore()
     peers = [(x_up, my), (x_dn, my), (mx, y_up), (mx, y_dn)] + [
-        partner(r, k) for r in range(rounds) for k in range(1, plan[r][1][1])
+        partner(r, k) for r in range(rounds) for k in range(1, radix)
     ]
     for peer in peers:
         pl.semaphore_signal(barrier, inc=1, device_id=peer, device_id_type=MESH)
@@ -199,7 +196,7 @@
                 src_ref=aro.at[r], dst_ref=ari.at[r, k - 1], send_sem=asend.at[r, k - 1],
                 recv_sem=arecv.at[r, k - 1], device_id=partner(r, k), device_id_type=MESH,
             )
-            for k in range(1, plan[r][1][1])
+            for k in range(1, radix)
         ]
 
     def send_sums(r):
@@ -300,9 +297,9 @@
             lambda x: ex[pl.ds(x * CY + row, 8), :],
             first + (part == 2), last - (part == 0),
         )
-        flux = joined(flux, part, edge, row)
+        flux = joined(flux, part, edge.at[s], row)
         for x in range(first, last):
-            tx[pl.ds(x * CY + row, 8), :] = flux[x - first] - flux[x - first + 1]
+            tx[s, pl.ds(x * CY + row, 8), :] = flux[x - first] - flux[x - first + 1]
 
     def y_faces(st, s, row, part):
         first, last = ((0, H), (H, CY - H), (CY - H, CY))[part]
@@ -311,92 +308,96 @@
             lambda y: ny[pl.ds(y * CX + row, 8), :],
             first + (part == 2), last - (part == 0),
         )
-        flux = joined(flux, part, edge, CY + row)
+        flux = joined(flux, part, edge.at[s], CY + row)
         for y in range(first, last):
-            ty[pl.ds(row * CY + y, 8, stride=CY), :] = flux[y - first] - flux[y - first + 1]
-
-    def z_faces(st, s):
-        def group(i, _):
-            first = pl.multiple_of(i * ZROWS, ZROWS)
-            rows = [pl.ds(first + 8 * v, 8) for v in range(ZROWS // 8)]
-            parts = [shifted_z(xs[st, s, pl.ds(H * CY + first + 8 * v, 8), :], lane) for v in range(ZROWS // 8)]
-            flux = [flux_z(uz[r, :], part, lane) for r, part in zip(rows, parts)]
-            for r, value in zip(rows, flux):
-                tz[r, :] = value - pltpu.roll(value, NZ - 1, 1)
-            return 0
-
-        lax.fori_loop(0, CELLS // ZROWS, group, 0)
-
-    def step(t, _):
-        st, s = lax.div(t, 2), lax.rem(t, 2)
-
-        def y_inner(i, _):
+            ty[s, pl.ds(row * CY + y, 8, stride=CY), :] = flux[y - first] - flux[y - first + 1]
+
+    def z_faces(st, s, first):
+        rows = [pl.ds(first + 8 * v, 8) for v in range(ZROWS // 8)]
+        parts = [shifted_z(xs[st, s, pl.ds(H * CY + first + 8 * v, 8), :], lane) for v in range(ZROWS // 8)]
+        flux = [flux_z(uz[r, :], part, lane) for r, part in zip(rows, parts)]
+        for r, value in zip(rows, flux):
+            tz[s, r, :] = value - pltpu.roll(value, NZ - 1, 1)
+
+    def columns(count, work, carry):
+        return lax.fori_loop(0, 2 * count, lambda i, c: work(lax.div(i, count), lax.rem(i, count), c), carry)
+
+    def stage(st, _):
+        def y_inner(s, i, _):
             y_faces(st, s, pl.multiple_of(i * 8, 8), 1)
             return 0
 
-        lax.fori_loop(0, CX // 8, y_inner, 0)
-
-        def x_inner(i, e):
+        def x_inner(s, i, e):
             x_faces(st, s, pl.multiple_of(i * 8, 8), 1)
-            return factor(t * PART + i * UNROLL, e)
-
-        es[...] = lax.fori_loop(0, CY // 8, x_inner, es[...])
-        z_faces(st, s)
-        for r, place in enumerate(PLACES[: rounds - 1]):
-
-            @pl.when(t == place)
-            def _(r=r):
-                add_sums(r)
-                send_sums(r + 1)
-
-
-        @pl.when(t == 0)
+            return factor(st * PART + (s * (CY // 8) + i) * UNROLL, e)
+
+        def z_all(s, i, _):
+            z_faces(st, s, pl.multiple_of(i * ZROWS, ZROWS))
+            return 0
+
+        columns(CX // 8, y_inner, 0)
+        es[...] = columns(CY // 8, x_inner, es[...])
+        columns(CELLS // ZROWS, z_all, 0)
+
+        @pl.when(st < rounds - 1)
+        def _():
+            add_sums(st)
+            send_sums(st + 1)
+
+        @pl.when(st == 0)
         def _():
             north_edge.wait_recv()
             east_edge.wait_recv()
 
-        halo(t, 2).wait_recv()
-        halo(t, 3).wait_recv()
-        for row in range(0, CX, 8):
-            y_faces(st, s, row, 0)
-            y_faces(st, s, row, 2)
-        halo(t, 0).wait_recv()
-        halo(t, 1).wait_recv()
-
-        def x_outer(i, _):
-            for k in range(2):
-                x_faces(st, s, pl.multiple_of(i * 16 + 8 * k, 8), 0)
-                x_faces(st, s, pl.multiple_of(i * 16 + 8 * k, 8), 2)
-            return 0
-
-        lax.fori_loop(0, CY // 16, x_outer, 0)
         coef = jnp.where(st == 0, STEP / 18.0, jnp.where(st == 1, STEP / 12.0, STEP / 6.0)).astype(jnp.float32)
 
-        def update(g, _):
-            rows = pl.ds(pl.multiple_of(g * GROUP * CY, CY), GROUP * CY)
-            value = bs[s, rows, :] + coef * (tx[rows, :] + ty[rows, :] + tz[rows, :])
+        def finish(s, _):
+            t = 2 * st + s
+
+            def y_outer(i, _):
+                y_faces(st, s, pl.multiple_of(i * 8, 8), 0)
+                y_faces(st, s, pl.multiple_of(i * 8, 8), 2)
+                return 0
+
+            def x_outer(i, _):
+                x_faces(st, s, pl.multiple_of(i * 8, 8), 0)
+                x_faces(st, s, pl.multiple_of(i * 8, 8), 2)
+                return 0
+
+            def update(g, _):
+                rows = pl.ds(pl.multiple_of(g * GROUP * CY, CY), GROUP * CY)
+                value = bs[s, rows, :] + coef * (tx[s, rows, :] + ty[s, rows, :] + tz[s, rows, :])
+
+                @pl.when(st < 2)
+                def _():
+                    xs[st + 1, s, pl.ds(pl.multiple_of((H + g * GROUP) * CY, CY), GROUP * CY), :] = value
+                    for p in range(GROUP):
+                        to_y(st + 1, s, g * GROUP + p, value[p * CY : (p + 1) * CY])
+
+                @pl.when(st == 2)
+                def _():
+                    adv[s, rows, :] = value
+
+                return 0
+
+            halo(t, 2).wait_recv()
+            halo(t, 3).wait_recv()
+            lax.fori_loop(0, CX // 8, y_outer, 0)
+            halo(t, 0).wait_recv()
+            halo(t, 1).wait_recv()
+            lax.fori_loop(0, CY // 8, x_outer, 0)
+            lax.fori_loop(0, CX // GROUP, update, 0)
 
             @pl.when(st < 2)
             def _():
-                xs[st + 1, s, pl.ds(pl.multiple_of((H + g * GROUP) * CY, CY), GROUP * CY), :] = value
-                for p in range(GROUP):
-                    to_y(st + 1, s, g * GROUP + p, value[p * CY : (p + 1) * CY])
-
-            @pl.when(st == 2)
-            def _():
-                adv[s, rows, :] = value
+                send_halos(t + 2, range(4))
 
             return 0
 
-        lax.fori_loop(0, CX // GROUP, update, 0)
-
-        @pl.when(st < 2)
-        def _():
-            send_halos(t + 2, range(4))
-
+        lax.fori_loop(0, 2, finish, 0)
         return 0
 
-    lax.fori_loop(0, 6, step, 0)
+    lax.fori_loop(0, 3, stage, 0)
 
     add_sums(rounds - 1)
     cells = float(n_x * CX * n_y * CY)
@@ -468,7 +469,7 @@
 
 
 def body(n_x, n_y, scalars, east_wind, north_wind, up_wind, diffusivity, target_profile):
-    rounds = len(digits(n_x)) + len(digits(n_y))
+    rounds = 2 * digits(n_x)[0]
     hbm = pl.BlockSpec(memory_space=pltpu.HBM)
     f32 = jnp.float32
     vmem = pltpu.VMEM
@@ -486,10 +487,10 @@
             vmem((3, 2, XROWS, NZ), f32),
             vmem((2, CELLS, NZ), f32),
             vmem((3, 2, YROWS, NZ), f32),
-            vmem((2, CY + CX, NZ), f32),
-            vmem((CELLS, NZ), f32),
-            vmem((CELLS, NZ), f32),
-            vmem((CELLS, NZ), f32),
+            vmem((2, 2, CY + CX, NZ), f32),
+            vmem((2, CELLS, NZ), f32),
+            vmem((2, CELLS, NZ), f32),
+            vmem((2, CELLS, NZ), f32),
             vmem((CELLS + CY, NZ), f32),
             vmem((CELLS + CX, NZ), f32),
             vmem((CELLS, NZ), f32),

time: 37.6 us -> 38 us (1.011)
  Pallas kernels: 37.5 us -> 37.9 us
where the time goes in v4:
time: 38 us; the launch traced here: 37.9 us
  Pallas kernels  37.9 us (100%)
    pallas_call x1, Pallas kernels, body(): pl.pallas_call(functools.partial(kernel, n_x, n_y), out_shape=[jax.ShapeD...  35.9 us
    pallas_call x1, Pallas kernels, body(): pl.pallas_call(solve, out_shape=jax.ShapeDtypeStruct((2, CELLS, NZ), f32)...  2.02 us

profile of v4, /device:TPU:1, one launch (start us, length us, event | category | flops | bytes accessed | tf_op | source)
XLA Modules:
  0.0 37.9 jit_solution(8555173477776318557)
XLA Ops:
  0.0 35.9 %shard_map.64 = (f32[2,768,128]{2,1,0:T(8,128)S(1)}, f32[2,128]{1,0:T(2,128)S(1)}, f32[1152,128]{1,0:T(8,128)S(1)}, f32[1152,128]{1,0:T(8,128)S(1)}, f32[1152,128]{1,0:T(8,128)S(1)}) custom-call(f32[2,768,128]{2,1,0:T(8,128)} %bitcast.6, f32[768,128]{1,0:T(8,128)} %bitcast.7, f32[768,128]{1,0:T(8,128)} %bitcast.8, f32[768,128]{1,0:T(8,128)} %bitcast.9, ...), custom_call_target="tpu_custom_call" | custom-call | flops 80000000 | bytes 4000000 | tf_op jit(solution)/shard_map/pallas_call | solution.py:479
  35.9 2.0 %shard_map.65 = f32[2,768,128]{2,1,0:T(8,128)} custom-call(f32[2,768,128]{2,1,0:T(8,128)S(1)} %get-tuple-element.10.adv, f32[2,128]{1,0:T(2,128)S(1)} %get-tuple-element.11.shift, f32[1152,128]{1,0:T(8,128)S(1)} %get-tuple-element.12.im, f32[1152,128]{1,0:T(8,128)S(1)} %get-tuple-element.13.av, f32[1152,128]{1,0:T(8,128)S(1)} %get-tuple-element.14.cp), custom_call_target="tpu_custom_call" | custom-call | flops 2000000 | bytes 4000000 | tf_op jit(solution)/shard_map/pallas_call | solution.py:524

commit v5 on v4

--- a/solution.py
+++ b/solution.py
@@ -15,12 +15,12 @@
 
 CX, CY, NZ = 24, 32, 128
 H = 3
-XROWS = (CX + 2 * H) * CY
 YROWS = (CY + 2 * H) * CX
 CELLS = CX * CY
 TILES = CELLS // 128
 GROUP = 8
 ZROWS = 192
+TURN = 16
 PART = 48
 LEVELS = 3 * PART
 UNROLL = PART // 8
@@ -51,7 +51,7 @@
     return u * (3.0 * total - gs) - jnp.abs(u) * part
 
 
-def march(load_f, load_u, first, last):
+def march(load_f, load_u, cells, emit):
     f, d, q, t = {}, {}, {}, {}
 
     def get_f(i):
@@ -75,27 +75,16 @@
             t[i] = get_q(i)[0] - get_q(i - 1)[0]
         return t[i]
 
-    out = []
-    for j in range(first, last + 1):
+    lower = None
+    for j in range(cells + 1):
         lo2, lo1, hi0, hi1 = get_q(j - 2), get_q(j - 1), get_q(j), get_q(j + 1)
-        out.append(
-            face(
-                load_u(j), get_f(j - 1) + get_f(j), lo1[0], hi0[0], get_t(j - 1), get_t(j), get_t(j + 1),
-                lo2[3], lo1[3], lo1[2], hi0[2], hi0[1], hi1[1],
-            )
+        upper = face(
+            load_u(j), get_f(j - 1) + get_f(j), lo1[0], hi0[0], get_t(j - 1), get_t(j), get_t(j + 1),
+            lo2[3], lo1[3], lo1[2], hi0[2], hi0[1], hi1[1],
         )
-    return out
-
-
-def joined(flux, part, edge, row):
-    rows = pl.ds(row, 8)
-    if part == 0:
-        return flux + [edge[0, rows, :]]
-    if part == 2:
-        return [edge[1, rows, :]] + flux
-    edge[0, rows, :] = flux[0]
-    edge[1, rows, :] = flux[-1]
-    return flux
+        if j > 0:
+            emit(j - 1, lower - upper)
+        lower = upper
 
 
 def shifted_z(f, lane):
@@ -138,8 +127,8 @@
 def kernel(
     n_x, n_y,
     scal, east, north, upw, diff, target, adv, shift, im, av, cp,
-    xs, bs, ys, edge, tz, tx, ty, ex, ny, nraw, uz, kd, tg, fk, es, aro, ari,
-    lsem, hsend, hrecv, wsend, wrecv, asend, arecv,
+    xf, xh, bs, ys, tz, ty, ex, ny, nraw, uz, kd, tg, fk, es, aro, ari,
+    lsem, csem, hsend, hrecv, wsend, wrecv, asend, arecv,
 ):
     mx, my = lax.axis_index("gx"), lax.axis_index("gy")
     x_up, x_dn = lax.rem(mx + 1, n_x), lax.rem(mx + n_x - 1, n_x)
@@ -155,8 +144,8 @@
         return on_x * other + (1 - on_x) * mx, on_x * my + (1 - on_x) * other
 
     loads = [
-        pltpu.make_async_copy(scal.at[0], xs.at[0, 0, pl.ds(H * CY, CELLS)], lsem.at[0]),
-        pltpu.make_async_copy(scal.at[1], xs.at[0, 1, pl.ds(H * CY, CELLS)], lsem.at[1]),
+        pltpu.make_async_copy(scal.at[0], xf.at[0], lsem.at[0]),
+        pltpu.make_async_copy(scal.at[1], xf.at[1], lsem.at[1]),
         pltpu.make_async_copy(north, nraw, lsem.at[2]),
         pltpu.make_async_copy(east, ex.at[pl.ds(0, CELLS)], lsem.at[3]),
         pltpu.make_async_copy(diff, kd, lsem.at[4]),
@@ -174,21 +163,18 @@
     for peer in peers:
         pl.semaphore_signal(barrier, inc=1, device_id=peer, device_id_type=MESH)
 
-    def halo(t, way):
+    def halo(t, way, field=adv):
         st, s = lax.div(t, 2), lax.rem(t, 2)
-        size = CY if way < 2 else CX
-        buffer, length = (xs, CX) if way < 2 else (ys, CY)
         to = ((x_up, my), (x_dn, my), (mx, y_up), (mx, y_dn))[way]
-        source, target_row = ((length, 0), (H, length + H))[way % 2]
+        if way < 2:
+            src, dst = field.at[s, pl.ds((CELLS - H * CY, 0)[way], H * CY)], xh.at[t, way]
+        else:
+            src = ys.at[st, s, pl.ds((CY, H)[way - 2] * CX, H * CX)]
+            dst = ys.at[st, s, pl.ds((0, CY + H)[way - 2] * CX, H * CX)]
         return pltpu.make_async_remote_copy(
-            src_ref=buffer.at[st, s, pl.ds(source * size, H * size)],
-            dst_ref=buffer.at[st, s, pl.ds(target_row * size, H * size)],
-            send_sem=hsend.at[t, way], recv_sem=hrecv.at[t, way], device_id=to, device_id_type=MESH,
+            src_ref=src, dst_ref=dst, send_sem=hsend.at[t, way], recv_sem=hrecv.at[t, way],
+            device_id=to, device_id_type=MESH,
         )
-
-    def send_halos(t, ways):
-        for way in ways:
-            halo(t, way).start()
 
     def exchange(r):
         return [
@@ -228,17 +214,19 @@
     pl.semaphore_wait(barrier, len(peers))
 
     def first_field(s, _):
-        send_halos(s, (0, 1))
+        halo(s, 0, xf).start()
+        halo(s, 1, xf).start()
 
         def convert(g, total):
-            values = [xs[0, s, pl.ds(pl.multiple_of((H + g * GROUP + p) * CY, CY), CY), :] for p in range(GROUP)]
+            values = [xf[s, pl.ds(pl.multiple_of((g * GROUP + p) * CY, CY), CY), :] for p in range(GROUP)]
             for p, value in enumerate(values):
                 to_y(0, s, g * GROUP + p, value)
             return total + sum(values)
 
         total = lax.fori_loop(0, CX // GROUP, convert, jnp.zeros((CY, NZ), jnp.float32))
         aro[0, pl.ds(s, 1), :] = jnp.sum(total, axis=0, keepdims=True)
-        send_halos(s, (2, 3))
+        halo(s, 2).start()
+        halo(s, 3).start()
         return 0
 
     lax.fori_loop(0, 2, first_field, 0)
@@ -270,7 +258,7 @@
         fk[pl.ds(c, NZ, stride=8), :] = jnp.transpose(kd[rows, :]) * STEP
         return 0
 
-    fk[...] = jnp.zeros(fk.shape, jnp.float32)
+    fk[pl.ds(NZ * 8, fk.shape[0] - NZ * 8), :] = jnp.zeros((fk.shape[0] - NZ * 8, 128), jnp.float32)
     lax.fori_loop(0, TILES, columns_to_lanes, 0)
     fk[pl.ds(0, 8), :] = jnp.zeros((8, 128), jnp.float32)
     es[...] = jnp.zeros((8, 128), jnp.float32)
@@ -290,54 +278,60 @@
             low = above
         return e
 
-    def x_faces(st, s, row, part):
-        first, last = ((0, H), (H, CX - H), (CX - H, CX))[part]
-        flux = march(
-            lambda x: xs[st, s, pl.ds((H + x) * CY + row, 8), :],
-            lambda x: ex[pl.ds(x * CY + row, 8), :],
-            first + (part == 2), last - (part == 0),
-        )
-        flux = joined(flux, part, edge.at[s], row)
-        for x in range(first, last):
-            tx[s, pl.ds(x * CY + row, 8), :] = flux[x - first] - flux[x - first + 1]
-
-    def y_faces(st, s, row, part):
-        first, last = ((0, H), (H, CY - H), (CY - H, CY))[part]
-        flux = march(
+    def y_column(st, s, row):
+        def keep(y, diff):
+            ty[pl.ds(row * CY + y, 8, stride=CY), :] = diff
+
+        march(
             lambda y: ys[st, s, pl.ds((H + y) * CX + row, 8), :],
             lambda y: ny[pl.ds(y * CX + row, 8), :],
-            first + (part == 2), last - (part == 0),
+            CY, keep,
         )
-        flux = joined(flux, part, edge.at[s], CY + row)
-        for y in range(first, last):
-            ty[s, pl.ds(row * CY + y, 8, stride=CY), :] = flux[y - first] - flux[y - first + 1]
-
-    def z_faces(st, s, first):
+
+    def x_column(st, s, row, coef):
+        t = 2 * st + s
+
+        def load(x):
+            if x < 0:
+                return xh[t, 0, pl.ds((x + H) * CY + row, 8), :]
+            if x >= CX:
+                return xh[t, 1, pl.ds((x - CX) * CY + row, 8), :]
+            return xf[s, pl.ds(x * CY + row, 8), :]
+
+        def keep(x, diff):
+            rows = pl.ds(x * CY + row, 8)
+            value = bs[s, rows, :] + coef * (diff + ty[rows, :] + tz[s, rows, :])
+            adv[s, rows, :] = value
+            ys[st + 1, s, pl.ds((H + row) * CX + x, 8, stride=CX), :] = value
+
+        march(load, lambda x: ex[pl.ds(x * CY + row, 8), :], CX, keep)
+
+    def z_faces(s, first):
         rows = [pl.ds(first + 8 * v, 8) for v in range(ZROWS // 8)]
-        parts = [shifted_z(xs[st, s, pl.ds(H * CY + first + 8 * v, 8), :], lane) for v in range(ZROWS // 8)]
+        parts = [shifted_z(xf[s, pl.ds(first + 8 * v, 8), :], lane) for v in range(ZROWS // 8)]
         flux = [flux_z(uz[r, :], part, lane) for r, part in zip(rows, parts)]
         for r, value in zip(rows, flux):
             tz[s, r, :] = value - pltpu.roll(value, NZ - 1, 1)
 
-    def columns(count, work, carry):
-        return lax.fori_loop(0, 2 * count, lambda i, c: work(lax.div(i, count), lax.rem(i, count), c), carry)
+    def back(s):
+        return pltpu.make_async_copy(adv.at[s], xf.at[s], csem.at[s])
 
     def stage(st, _):
-        def y_inner(s, i, _):
-            y_faces(st, s, pl.multiple_of(i * 8, 8), 1)
+        coef = jnp.where(st == 0, STEP / 18.0, jnp.where(st == 1, STEP / 12.0, STEP / 6.0)).astype(jnp.float32)
+
+        def z_pass(s, _):
+            @pl.when(st > 0)
+            def _():
+                back(s).wait()
+
+            def group(i, _):
+                z_faces(s, pl.multiple_of(i * ZROWS, ZROWS))
+                return 0
+
+            lax.fori_loop(0, CELLS // ZROWS, group, 0)
             return 0
 
-        def x_inner(s, i, e):
-            x_faces(st, s, pl.multiple_of(i * 8, 8), 1)
-            return factor(st * PART + (s * (CY // 8) + i) * UNROLL, e)
-
-        def z_all(s, i, _):
-            z_faces(st, s, pl.multiple_of(i * ZROWS, ZROWS))
-            return 0
-
-        columns(CX // 8, y_inner, 0)
-        es[...] = columns(CY // 8, x_inner, es[...])
-        columns(CELLS // ZROWS, z_all, 0)
+        lax.fori_loop(0, 2, z_pass, 0)
 
         @pl.when(st < rounds - 1)
         def _():
@@ -349,48 +343,30 @@
             north_edge.wait_recv()
             east_edge.wait_recv()
 
-        coef = jnp.where(st == 0, STEP / 18.0, jnp.where(st == 1, STEP / 12.0, STEP / 6.0)).astype(jnp.float32)
-
         def finish(s, _):
             t = 2 * st + s
 
-            def y_outer(i, _):
-                y_faces(st, s, pl.multiple_of(i * 8, 8), 0)
-                y_faces(st, s, pl.multiple_of(i * 8, 8), 2)
+            def y_pass(i, _):
+                y_column(st, s, pl.multiple_of(i * 8, 8))
                 return 0
 
-            def x_outer(i, _):
-                x_faces(st, s, pl.multiple_of(i * 8, 8), 0)
-                x_faces(st, s, pl.multiple_of(i * 8, 8), 2)
-                return 0
-
-            def update(g, _):
-                rows = pl.ds(pl.multiple_of(g * GROUP * CY, CY), GROUP * CY)
-                value = bs[s, rows, :] + coef * (tx[s, rows, :] + ty[s, rows, :] + tz[s, rows, :])
-
-                @pl.when(st < 2)
-                def _():
-                    xs[st + 1, s, pl.ds(pl.multiple_of((H + g * GROUP) * CY, CY), GROUP * CY), :] = value
-                    for p in range(GROUP):
-                        to_y(st + 1, s, g * GROUP + p, value[p * CY : (p + 1) * CY])
-
-                @pl.when(st == 2)
-                def _():
-                    adv[s, rows, :] = value
-
-                return 0
+            def x_pass(i, e):
+                x_column(st, s, pl.multiple_of(i * 8, 8), coef)
+                return factor(st * PART + (s * (CY // 8) + i) * UNROLL, e)
 
             halo(t, 2).wait_recv()
             halo(t, 3).wait_recv()
-            lax.fori_loop(0, CX // 8, y_outer, 0)
-            halo(t, 0).wait_recv()
-            halo(t, 1).wait_recv()
-            lax.fori_loop(0, CY // 8, x_outer, 0)
-            lax.fori_loop(0, CX // GROUP, update, 0)
+            lax.fori_loop(0, CX // 8, y_pass, 0)
+            for way in range(2):
+                halo(t, way).wait_recv()
+                halo(t, way).wait_send()
+            es[...] = lax.fori_loop(0, CY // 8, x_pass, es[...])
 
             @pl.when(st < 2)
             def _():
-                send_halos(t + 2, range(4))
+                for way in (2, 3, 0, 1):
+                    halo(t + 2, way).start()
+                back(s).start()
 
             return 0
 
@@ -404,7 +380,7 @@
     shift[...] = RELAX * (aro[rounds] * (1.0 / cells) - tg[...])
 
     def drain(t, _):
-        for way in range(4):
+        for way in (2, 3):
             halo(t, way).wait_send()
         return 0
 
@@ -427,8 +403,8 @@
 
     def forward(k8, carry):
         d0, d1 = carry
-        base = pl.multiple_of(k8 * 64, 64)
-        rows = [pl.ds(base + 8 * i, 8) for i in range(8)]
+        base = pl.multiple_of(k8 * (TURN * 8), TURN * 8)
+        rows = [pl.ds(base + 8 * i, 8) for i in range(TURN)]
         data = [(im[r, :], av[r, :], rh[0, r, :], rh[1, r, :]) for r in rows]
         for i, (inverse, a, r0, r1) in enumerate(data):
             d0 = r0 * inverse + a * d0
@@ -437,12 +413,12 @@
             rh[1, rows[i], :] = d1
         return d0, d1
 
-    lax.fori_loop(0, NZ // 8, forward, (zero, zero))
+    lax.fori_loop(0, NZ // TURN, forward, (zero, zero))
 
     def backward(j8, carry):
         v0, v1 = carry
-        base = pl.multiple_of((NZ // 8 - 1 - j8) * 64, 64)
-        rows = [pl.ds(base + 56 - 8 * i, 8) for i in range(8)]
+        base = pl.multiple_of((NZ // TURN - 1 - j8) * (TURN * 8), TURN * 8)
+        rows = [pl.ds(base + 8 * (TURN - 1 - i), 8) for i in range(TURN)]
         data = [(cp[r, :], rh[0, r, :], rh[1, r, :]) for r in rows]
         for i, (c, r0, r1) in enumerate(data):
             v0 = r0 + c * v0
@@ -451,7 +427,7 @@
             rh[1, rows[i], :] = v1
         return v0, v1
 
-    lax.fori_loop(0, NZ // 8, backward, (zero, zero))
+    lax.fori_loop(0, NZ // TURN, backward, (zero, zero))
     stores = []
     for s in range(2):
         for c in range(TILES):
@@ -484,13 +460,12 @@
         in_specs=[hbm] * 6,
         out_specs=[resident] * 5,
         scratch_shapes=[
-            vmem((3, 2, XROWS, NZ), f32),
             vmem((2, CELLS, NZ), f32),
-            vmem((3, 2, YROWS, NZ), f32),
-            vmem((2, 2, CY + CX, NZ), f32),
+            vmem((6, 2, H * CY, NZ), f32),
             vmem((2, CELLS, NZ), f32),
+            vmem((4, 2, YROWS, NZ), f32),
             vmem((2, CELLS, NZ), f32),
-            vmem((2, CELLS, NZ), f32),
+            vmem((CELLS, NZ), f32),
             vmem((CELLS + CY, NZ), f32),
             vmem((CELLS + CX, NZ), f32),
             vmem((CELLS, NZ), f32),
@@ -502,6 +477,7 @@
             vmem((rounds + 1, 2, NZ), f32),
             vmem((rounds, 3, 2, NZ), f32),
             dma((8,)),
+            dma((2,)),
             dma((6, 4)),
             dma((6, 4)),
             dma((2,)),

time: 38 us -> 37.7 us (level)
  no operation moved by 1% of the time
where the time goes in v5:
time: 37.7 us; the launch traced here: 37.6 us
  Pallas kernels  37.6 us (100%)
    pallas_call x1, Pallas kernels, body(): pl.pallas_call(functools.partial(kernel, n_x, n_y), out_shape=[jax.ShapeD...  35.7 us
    pallas_call x1, Pallas kernels, body(): pl.pallas_call(solve, out_shape=jax.ShapeDtypeStruct((2, CELLS, NZ), f32)...  1.95 us

profile of v5, /device:TPU:1, one launch (start us, length us, event | category | flops | bytes accessed | tf_op | source)
XLA Modules:
  0.0 37.6 jit_solution(9813584393369040254)
XLA Ops:
  0.0 35.7 %shard_map.64 = (f32[2,768,128]{2,1,0:T(8,128)S(1)}, f32[2,128]{1,0:T(2,128)S(1)}, f32[1152,128]{1,0:T(8,128)S(1)}, f32[1152,128]{1,0:T(8,128)S(1)}, f32[1152,128]{1,0:T(8,128)S(1)}) custom-call(f32[2,768,128]{2,1,0:T(8,128)} %bitcast.6, f32[768,128]{1,0:T(8,128)} %bitcast.7, f32[768,128]{1,0:T(8,128)} %bitcast.8, f32[768,128]{1,0:T(8,128)} %bitcast.9, ...), custom_call_target="tpu_custom_call" | custom-call | flops 80000000 | bytes 4000000 | tf_op jit(solution)/shard_map/pallas_call | solution.py:455
  35.7 2.0 %shard_map.65 = f32[2,768,128]{2,1,0:T(8,128)} custom-call(f32[2,768,128]{2,1,0:T(8,128)S(1)} %get-tuple-element.10.adv, f32[2,128]{1,0:T(2,128)S(1)} %get-tuple-element.11.shift, f32[1152,128]{1,0:T(8,128)S(1)} %get-tuple-element.12.im, f32[1152,128]{1,0:T(8,128)S(1)} %get-tuple-element.13.av, f32[1152,128]{1,0:T(8,128)S(1)} %get-tuple-element.14.cp), custom_call_target="tpu_custom_call" | custom-call | flops 2000000 | bytes 4000000 | tf_op jit(solution)/shard_map/pallas_call | solution.py:500

commit v6 on v5

--- a/solution.py
+++ b/solution.py
@@ -196,6 +196,12 @@
             total = total + ari[r, k]
         aro[r + 1] = total
 
+    def next_sums(r):
+        @pl.when(r < rounds - 1)
+        def _():
+            add_sums(r)
+            send_sums(r + 1)
+
     east_edge = pltpu.make_async_remote_copy(
         src_ref=ex.at[pl.ds(0, CY)], dst_ref=ex.at[pl.ds(CELLS, CY)], send_sem=wsend.at[0], recv_sem=wrecv.at[0],
         device_id=(x_dn, my), device_id_type=MESH,
@@ -333,10 +339,7 @@
 
         lax.fori_loop(0, 2, z_pass, 0)
 
-        @pl.when(st < rounds - 1)
-        def _():
-            add_sums(st)
-            send_sums(st + 1)
+        next_sums(2 * st)
 
         @pl.when(st == 0)
         def _():
@@ -371,6 +374,7 @@
             return 0
 
         lax.fori_loop(0, 2, finish, 0)
+        next_sums(2 * st + 1)
         return 0
 
     lax.fori_loop(0, 3, stage, 0)

time: 37.7 us -> 39.6 us (1.050)
  Pallas kernels: 37.6 us -> 39.5 us
    pallas_call x1, Pallas kernels: 35.7 us -> 37.5 us  [body(): pl.pallas_call(functools.partial(kernel, n_x, n_y), out_shape=[jax.ShapeD...]
where the time goes in v6:
time: 39.6 us; the launch traced here: 39.5 us
  Pallas kernels  39.5 us (100%)
    pallas_call x1, Pallas kernels, body(): pl.pallas_call(functools.partial(kernel, n_x, n_y), out_shape=[jax.ShapeD...  37.5 us
    pallas_call x1, Pallas kernels, body(): pl.pallas_call(solve, out_shape=jax.ShapeDtypeStruct((2, CELLS, NZ), f32)...  1.95 us

profile of v6, /device:TPU:1, one launch (start us, length us, event | category | flops | bytes accessed | tf_op | source)
XLA Modules:
  0.0 39.5 jit_solution(9920322845835422681)
XLA Ops:
  0.0 37.5 %shard_map.64 = (f32[2,768,128]{2,1,0:T(8,128)S(1)}, f32[2,128]{1,0:T(2,128)S(1)}, f32[1152,128]{1,0:T(8,128)S(1)}, f32[1152,128]{1,0:T(8,128)S(1)}, f32[1152,128]{1,0:T(8,128)S(1)}) custom-call(f32[2,768,128]{2,1,0:T(8,128)} %bitcast.6, f32[768,128]{1,0:T(8,128)} %bitcast.7, f32[768,128]{1,0:T(8,128)} %bitcast.8, f32[768,128]{1,0:T(8,128)} %bitcast.9, ...), custom_call_target="tpu_custom_call" | custom-call | flops 80000000 | bytes 4000000 | tf_op jit(solution)/shard_map/pallas_call | solution.py:459
  37.5 2.0 %shard_map.65 = f32[2,768,128]{2,1,0:T(8,128)} custom-call(f32[2,768,128]{2,1,0:T(8,128)S(1)} %get-tuple-element.10.adv, f32[2,128]{1,0:T(2,128)S(1)} %get-tuple-element.11.shift, f32[1152,128]{1,0:T(8,128)S(1)} %get-tuple-element.12.im, f32[1152,128]{1,0:T(8,128)S(1)} %get-tuple-element.13.av, f32[1152,128]{1,0:T(8,128)S(1)} %get-tuple-element.14.cp), custom_call_target="tpu_custom_call" | custom-call | flops 2000000 | bytes 4000000 | tf_op jit(solution)/shard_map/pallas_call | solution.py:504

commit v7 on v5

--- a/solution.py
+++ b/solution.py
@@ -118,10 +118,11 @@
 
 
 def digits(n):
-    radix, count = min(4, n), 1
-    while radix**count < n:
-        count += 1
-    return count, radix
+    out, stride = [], 1
+    while stride < n:
+        out.append((stride, min(4, n // stride)))
+        stride *= out[-1][1]
+    return out
 
 
 def kernel(
@@ -133,15 +134,22 @@
     mx, my = lax.axis_index("gx"), lax.axis_index("gy")
     x_up, x_dn = lax.rem(mx + 1, n_x), lax.rem(mx + n_x - 1, n_x)
     y_up, y_dn = lax.rem(my + 1, n_y), lax.rem(my + n_y - 1, n_y)
-    per_axis, radix = digits(n_x)
-    rounds = 2 * per_axis
+    plan = digits(n_x) + [(1, n_y)]
+    rounds = len(plan)
 
     def partner(r, k):
-        on_x, stride = 1 - r // per_axis, 1 + (r % per_axis) * (radix - 1)
-        me = on_x * mx + (1 - on_x) * my
-        digit = lax.rem(lax.div(me, stride), radix)
-        other = me + stride * (lax.rem(digit + k, radix) - digit)
-        return on_x * other + (1 - on_x) * mx, on_x * my + (1 - on_x) * other
+        stride, size = plan[r]
+        me = my if r == rounds - 1 else mx
+        digit = lax.rem(lax.div(me, stride), size)
+        other = me + stride * (lax.rem(digit + k, size) - digit)
+        return (mx, other) if r == rounds - 1 else (other, my)
+
+    def for_peers(r, work):
+        def one(k, _):
+            work(k)
+            return 0
+
+        lax.fori_loop(1, plan[r][1], one, 0)
 
     loads = [
         pltpu.make_async_copy(scal.at[0], xf.at[0], lsem.at[0]),
@@ -158,10 +166,14 @@
 
     barrier = pltpu.get_barrier_semaphore()
     peers = [(x_up, my), (x_dn, my), (mx, y_up), (mx, y_dn)] + [
-        partner(r, k) for r in range(rounds) for k in range(1, radix)
+        partner(r, k) for r in range(rounds - 1) for k in range(1, plan[r][1])
     ]
+    def greet(peer):
+        pl.semaphore_signal(barrier, inc=1, device_id=peer, device_id_type=MESH)
+
     for peer in peers:
-        pl.semaphore_signal(barrier, inc=1, device_id=peer, device_id_type=MESH)
+        greet(peer)
+    for_peers(rounds - 1, lambda k: greet(partner(rounds - 1, k)))
 
     def halo(t, way, field=adv):
         st, s = lax.div(t, 2), lax.rem(t, 2)
@@ -176,25 +188,21 @@
             device_id=to, device_id_type=MESH,
         )
 
-    def exchange(r):
-        return [
-            pltpu.make_async_remote_copy(
-                src_ref=aro.at[r], dst_ref=ari.at[r, k - 1], send_sem=asend.at[r, k - 1],
-                recv_sem=arecv.at[r, k - 1], device_id=partner(r, k), device_id_type=MESH,
-            )
-            for k in range(1, radix)
-        ]
+    def exchange(r, k):
+        return pltpu.make_async_remote_copy(
+            src_ref=aro.at[r], dst_ref=ari.at[r, k - 1], send_sem=asend.at[r, k - 1],
+            recv_sem=arecv.at[r, k - 1], device_id=partner(r, k), device_id_type=MESH,
+        )
 
     def send_sums(r):
-        for copy in exchange(r):
-            copy.start()
+        for_peers(r, lambda k: exchange(r, k).start())
 
     def add_sums(r):
-        total = aro[r]
-        for k, copy in enumerate(exchange(r)):
-            copy.wait_recv()
-            total = total + ari[r, k]
-        aro[r + 1] = total
+        def add(k, total):
+            exchange(r, k).wait_recv()
+            return total + ari[r, k - 1]
+
+        aro[r + 1] = lax.fori_loop(1, plan[r][1], add, aro[r])
 
     east_edge = pltpu.make_async_remote_copy(
         src_ref=ex.at[pl.ds(0, CY)], dst_ref=ex.at[pl.ds(CELLS, CY)], send_sem=wsend.at[0], recv_sem=wrecv.at[0],
@@ -211,7 +219,7 @@
 
     loads[0].wait()
     loads[1].wait()
-    pl.semaphore_wait(barrier, len(peers))
+    pl.semaphore_wait(barrier, len(peers) + n_y - 1)
 
     def first_field(s, _):
         halo(s, 0, xf).start()
@@ -333,10 +341,12 @@
 
         lax.fori_loop(0, 2, z_pass, 0)
 
-        @pl.when(st < rounds - 1)
-        def _():
-            add_sums(st)
-            send_sums(st + 1)
+        for r in range(rounds - 1):
+
+            @pl.when(st == r)
+            def _(r=r):
+                add_sums(r)
+                send_sums(r + 1)
 
         @pl.when(st == 0)
         def _():
@@ -387,8 +397,7 @@
     lax.fori_loop(0, 6, drain, 0)
 
     for r in range(rounds):
-        for copy in exchange(r):
-            copy.wait_send()
+        for_peers(r, lambda k, r=r: exchange(r, k).wait_send())
     east_edge.wait_send()
     north_edge.wait_send()
 
@@ -445,7 +454,7 @@
 
 
 def body(n_x, n_y, scalars, east_wind, north_wind, up_wind, diffusivity, target_profile):
-    rounds = 2 * digits(n_x)[0]
+    rounds = len(digits(n_x)) + 1
     hbm = pl.BlockSpec(memory_space=pltpu.HBM)
     f32 = jnp.float32
     vmem = pltpu.VMEM
@@ -475,15 +484,15 @@
             vmem(((LEVELS + 1) * 8, 128), f32),
             vmem((8, 128), f32),
             vmem((rounds + 1, 2, NZ), f32),
-            vmem((rounds, 3, 2, NZ), f32),
+            vmem((rounds, n_y - 1, 2, NZ), f32),
             dma((8,)),
             dma((2,)),
             dma((6, 4)),
             dma((6, 4)),
             dma((2,)),
             dma((2,)),
-            dma((rounds, 3)),
-            dma((rounds, 3)),
+            dma((rounds, n_y - 1)),
+            dma((rounds, n_y - 1)),
         ],
         compiler_params=pltpu.CompilerParams(
             collective_id=0, has_side_effects=True, vmem_limit_bytes=48 * 1024 * 1024

time: 37.7 us -> 39.4 us (1.045)
  Pallas kernels: 37.6 us -> 39.3 us
    pallas_call x1, Pallas kernels: 35.7 us -> 37.4 us  [body(): pl.pallas_call(functools.partial(kernel, n_x, n_y), out_shape=[jax.ShapeD...]
where the time goes in v7:
time: 39.4 us; the launch traced here: 39.3 us
  Pallas kernels  39.3 us (100%)
    pallas_call x1, Pallas kernels, body(): pl.pallas_call(functools.partial(kernel, n_x, n_y), out_shape=[jax.ShapeD...  37.4 us
    pallas_call x1, Pallas kernels, body(): pl.pallas_call(solve, out_shape=jax.ShapeDtypeStruct((2, CELLS, NZ), f32)...  1.95 us

profile of v7, /device:TPU:1, one launch (start us, length us, event | category | flops | bytes accessed | tf_op | source)
XLA Modules:
  0.0 39.3 jit_solution(2380089977590689216)
XLA Ops:
  0.0 37.4 %shard_map.64 = (f32[2,768,128]{2,1,0:T(8,128)S(1)}, f32[2,128]{1,0:T(2,128)S(1)}, f32[1152,128]{1,0:T(8,128)S(1)}, f32[1152,128]{1,0:T(8,128)S(1)}, f32[1152,128]{1,0:T(8,128)S(1)}) custom-call(f32[2,768,128]{2,1,0:T(8,128)} %bitcast.6, f32[768,128]{1,0:T(8,128)} %bitcast.7, f32[768,128]{1,0:T(8,128)} %bitcast.8, f32[768,128]{1,0:T(8,128)} %bitcast.9, ...), custom_call_target="tpu_custom_call" | custom-call | flops 80000000 | bytes 4000000 | tf_op jit(solution)/shard_map/pallas_call | solution.py:464
  37.4 2.0 %shard_map.65 = f32[2,768,128]{2,1,0:T(8,128)} custom-call(f32[2,768,128]{2,1,0:T(8,128)S(1)} %get-tuple-element.10.adv, f32[2,128]{1,0:T(2,128)S(1)} %get-tuple-element.11.shift, f32[1152,128]{1,0:T(8,128)S(1)} %get-tuple-element.12.im, f32[1152,128]{1,0:T(8,128)S(1)} %get-tuple-element.13.av, f32[1152,128]{1,0:T(8,128)S(1)} %get-tuple-element.14.cp), custom_call_target="tpu_custom_call" | custom-call | flops 2000000 | bytes 4000000 | tf_op jit(solution)/shard_map/pallas_call | solution.py:509

commit v8 on v5

--- a/solution.py
+++ b/solution.py
@@ -118,10 +118,12 @@
 
 
 def digits(n):
-    radix, count = min(4, n), 1
-    while radix**count < n:
-        count += 1
-    return count, radix
+    out, stride = [], 1
+    while stride < n:
+        radix = min(4, n // stride)
+        out.append((stride, radix))
+        stride *= radix
+    return out
 
 
 def kernel(
@@ -133,15 +135,15 @@
     mx, my = lax.axis_index("gx"), lax.axis_index("gy")
     x_up, x_dn = lax.rem(mx + 1, n_x), lax.rem(mx + n_x - 1, n_x)
     y_up, y_dn = lax.rem(my + 1, n_y), lax.rem(my + n_y - 1, n_y)
-    per_axis, radix = digits(n_x)
-    rounds = 2 * per_axis
+    plan = [("x", d) for d in digits(n_x)] + [("y", d) for d in digits(n_y)]
+    rounds = len(plan)
 
     def partner(r, k):
-        on_x, stride = 1 - r // per_axis, 1 + (r % per_axis) * (radix - 1)
-        me = on_x * mx + (1 - on_x) * my
+        axis, (stride, radix) = plan[r]
+        me = mx if axis == "x" else my
         digit = lax.rem(lax.div(me, stride), radix)
         other = me + stride * (lax.rem(digit + k, radix) - digit)
-        return on_x * other + (1 - on_x) * mx, on_x * my + (1 - on_x) * other
+        return (other, my) if axis == "x" else (mx, other)
 
     loads = [
         pltpu.make_async_copy(scal.at[0], xf.at[0], lsem.at[0]),
@@ -158,7 +160,7 @@
 
     barrier = pltpu.get_barrier_semaphore()
     peers = [(x_up, my), (x_dn, my), (mx, y_up), (mx, y_dn)] + [
-        partner(r, k) for r in range(rounds) for k in range(1, radix)
+        partner(r, k) for r in range(rounds) for k in range(1, plan[r][1][1])
     ]
     for peer in peers:
         pl.semaphore_signal(barrier, inc=1, device_id=peer, device_id_type=MESH)
@@ -182,7 +184,7 @@
                 src_ref=aro.at[r], dst_ref=ari.at[r, k - 1], send_sem=asend.at[r, k - 1],
                 recv_sem=arecv.at[r, k - 1], device_id=partner(r, k), device_id_type=MESH,
             )
-            for k in range(1, radix)
+            for k in range(1, plan[r][1][1])
         ]
 
     def send_sums(r):
@@ -333,10 +335,12 @@
 
         lax.fori_loop(0, 2, z_pass, 0)
 
-        @pl.when(st < rounds - 1)
-        def _():
-            add_sums(st)
-            send_sums(st + 1)
+        for r in range(rounds - 1):
+
+            @pl.when(st == r)
+            def _(r=r):
+                add_sums(r)
+                send_sums(r + 1)
 
         @pl.when(st == 0)
         def _():
@@ -364,7 +368,7 @@
 
             @pl.when(st < 2)
             def _():
-                for way in (2, 3, 0, 1):
+                for way in range(4):
                     halo(t + 2, way).start()
                 back(s).start()
 
@@ -445,7 +449,7 @@
 
 
 def body(n_x, n_y, scalars, east_wind, north_wind, up_wind, diffusivity, target_profile):
-    rounds = 2 * digits(n_x)[0]
+    rounds = len(digits(n_x)) + len(digits(n_y))
     hbm = pl.BlockSpec(memory_space=pltpu.HBM)
     f32 = jnp.float32
     vmem = pltpu.VMEM

time: 37.7 us -> 38.2 us (1.013)
  Pallas kernels: 37.6 us -> 38.1 us
    pallas_call x1, Pallas kernels: 35.7 us -> 36.2 us  [body(): pl.pallas_call(functools.partial(kernel, n_x, n_y), out_shape=[jax.ShapeD...]
where the time goes in v8:
time: 38.2 us; the launch traced here: 38.1 us
  Pallas kernels  38.1 us (100%)
    pallas_call x1, Pallas kernels, body(): pl.pallas_call(functools.partial(kernel, n_x, n_y), out_shape=[jax.ShapeD...  36.2 us
    pallas_call x1, Pallas kernels, body(): pl.pallas_call(solve, out_shape=jax.ShapeDtypeStruct((2, CELLS, NZ), f32)...  1.95 us

profile of v8, /device:TPU:1, one launch (start us, length us, event | category | flops | bytes accessed | tf_op | source)
XLA Modules:
  0.0 38.1 jit_solution(11797119381208802300)
XLA Ops:
  0.0 36.2 %shard_map.64 = (f32[2,768,128]{2,1,0:T(8,128)S(1)}, f32[2,128]{1,0:T(2,128)S(1)}, f32[1152,128]{1,0:T(8,128)S(1)}, f32[1152,128]{1,0:T(8,128)S(1)}, f32[1152,128]{1,0:T(8,128)S(1)}) custom-call(f32[2,768,128]{2,1,0:T(8,128)} %bitcast.6, f32[768,128]{1,0:T(8,128)} %bitcast.7, f32[768,128]{1,0:T(8,128)} %bitcast.8, f32[768,128]{1,0:T(8,128)} %bitcast.9, ...), custom_call_target="tpu_custom_call" | custom-call | flops 80000000 | bytes 4000000 | tf_op jit(solution)/shard_map/pallas_call | solution.py:459
  36.2 2.0 %shard_map.65 = f32[2,768,128]{2,1,0:T(8,128)} custom-call(f32[2,768,128]{2,1,0:T(8,128)S(1)} %get-tuple-element.10.adv, f32[2,128]{1,0:T(2,128)S(1)} %get-tuple-element.11.shift, f32[1152,128]{1,0:T(8,128)S(1)} %get-tuple-element.12.im, f32[1152,128]{1,0:T(8,128)S(1)} %get-tuple-element.13.av, f32[1152,128]{1,0:T(8,128)S(1)} %get-tuple-element.14.cp), custom_call_target="tpu_custom_call" | custom-call | flops 2000000 | bytes 4000000 | tf_op jit(solution)/shard_map/pallas_call | solution.py:504

commit v9 on v5

--- a/solution.py
+++ b/solution.py
@@ -163,11 +163,12 @@
     for peer in peers:
         pl.semaphore_signal(barrier, inc=1, device_id=peer, device_id_type=MESH)
 
-    def halo(t, way, field=adv):
+    def halo(t, way, field=adv, row=None):
         st, s = lax.div(t, 2), lax.rem(t, 2)
         to = ((x_up, my), (x_dn, my), (mx, y_up), (mx, y_dn))[way]
         if way < 2:
-            src, dst = field.at[s, pl.ds((CELLS - H * CY, 0)[way], H * CY)], xh.at[t, way]
+            rows = pl.ds(0, CY) if row is None else pl.ds(row, 8)
+            src, dst = field.at[s, pl.ds((CX - H, 0)[way], H), rows], xh.at[t, way, :, rows]
         else:
             src = ys.at[st, s, pl.ds((CY, H)[way - 2] * CX, H * CX)]
             dst = ys.at[st, s, pl.ds((0, CY + H)[way - 2] * CX, H * CX)]
@@ -218,7 +219,7 @@
         halo(s, 1, xf).start()
 
         def convert(g, total):
-            values = [xf[s, pl.ds(pl.multiple_of((g * GROUP + p) * CY, CY), CY), :] for p in range(GROUP)]
+            values = [xf[s, g * GROUP + p] for p in range(GROUP)]
             for p, value in enumerate(values):
                 to_y(0, s, g * GROUP + p, value)
             return total + sum(values)
@@ -293,22 +294,24 @@
 
         def load(x):
             if x < 0:
-                return xh[t, 0, pl.ds((x + H) * CY + row, 8), :]
+                return xh[t, 0, x + H, pl.ds(row, 8), :]
             if x >= CX:
-                return xh[t, 1, pl.ds((x - CX) * CY + row, 8), :]
-            return xf[s, pl.ds(x * CY + row, 8), :]
+                return xh[t, 1, x - CX, pl.ds(row, 8), :]
+            return xf[s, x, pl.ds(row, 8), :]
 
         def keep(x, diff):
             rows = pl.ds(x * CY + row, 8)
-            value = bs[s, rows, :] + coef * (diff + ty[rows, :] + tz[s, rows, :])
-            adv[s, rows, :] = value
+            value = bs[s, x, pl.ds(row, 8), :] + coef * (diff + ty[rows, :] + tz[s, rows, :])
+            adv[s, x, pl.ds(row, 8), :] = value
             ys[st + 1, s, pl.ds((H + row) * CX + x, 8, stride=CX), :] = value
 
         march(load, lambda x: ex[pl.ds(x * CY + row, 8), :], CX, keep)
 
-    def z_faces(s, first):
-        rows = [pl.ds(first + 8 * v, 8) for v in range(ZROWS // 8)]
-        parts = [shifted_z(xf[s, pl.ds(first + 8 * v, 8), :], lane) for v in range(ZROWS // 8)]
+    def z_faces(s, group):
+        planes = ZROWS // CY
+        x = [group * planes + v // (CY // 8) for v in range(ZROWS // 8)]
+        rows = [pl.ds(pl.multiple_of(group * ZROWS, ZROWS) + 8 * v, 8) for v in range(ZROWS // 8)]
+        parts = [shifted_z(xf[s, x[v], pl.ds(8 * v % CY, 8), :], lane) for v in range(ZROWS // 8)]
         flux = [flux_z(uz[r, :], part, lane) for r, part in zip(rows, parts)]
         for r, value in zip(rows, flux):
             tz[s, r, :] = value - pltpu.roll(value, NZ - 1, 1)
@@ -325,7 +328,7 @@
                 back(s).wait()
 
             def group(i, _):
-                z_faces(s, pl.multiple_of(i * ZROWS, ZROWS))
+                z_faces(s, i)
                 return 0
 
             lax.fori_loop(0, CELLS // ZROWS, group, 0)
@@ -351,8 +354,24 @@
                 return 0
 
             def x_pass(i, e):
-                x_column(st, s, pl.multiple_of(i * 8, 8), coef)
-                return factor(st * PART + (s * (CY // 8) + i) * UNROLL, e)
+                row = pl.multiple_of(i * 8, 8)
+                x_column(st, s, row, coef)
+                e = factor(st * PART + (s * (CY // 8) + i) * UNROLL, e)
+
+                @pl.when(st < 2)
+                def _():
+                    halo(t + 2, 0, row=row).start()
+                    halo(t + 2, 1, row=row).start()
+
+                    @pl.when(i == 0)
+                    def _():
+                        halo(t + 2, 3).start()
+
+                    @pl.when(i == CY // 8 - 1)
+                    def _():
+                        halo(t + 2, 2).start()
+
+                return e
 
             halo(t, 2).wait_recv()
             halo(t, 3).wait_recv()
@@ -364,8 +383,6 @@
 
             @pl.when(st < 2)
             def _():
-                for way in (2, 3, 0, 1):
-                    halo(t + 2, way).start()
                 back(s).start()
 
             return 0
@@ -455,14 +472,14 @@
     parts = pl.pallas_call(
         functools.partial(kernel, n_x, n_y),
         out_shape=[
-            jax.ShapeDtypeStruct((2, CELLS, NZ), f32), jax.ShapeDtypeStruct((2, NZ), f32), columns, columns, columns,
+            jax.ShapeDtypeStruct((2, CX, CY, NZ), f32), jax.ShapeDtypeStruct((2, NZ), f32), columns, columns, columns,
         ],
         in_specs=[hbm] * 6,
         out_specs=[resident] * 5,
         scratch_shapes=[
-            vmem((2, CELLS, NZ), f32),
-            vmem((6, 2, H * CY, NZ), f32),
-            vmem((2, CELLS, NZ), f32),
+            vmem((2, CX, CY, NZ), f32),
+            vmem((6, 2, H, CY, NZ), f32),
+            vmem((2, CX, CY, NZ), f32),
             vmem((4, 2, YROWS, NZ), f32),
             vmem((2, CELLS, NZ), f32),
             vmem((CELLS, NZ), f32),
@@ -490,7 +507,7 @@
         ),
         cost_estimate=pl.CostEstimate(flops=80_000_000, bytes_accessed=4_000_000, transcendentals=0),
     )(
-        in_hbm(scalars.reshape(2, CELLS, NZ)),
+        in_hbm(scalars),
         in_hbm(east_wind.reshape(CELLS, NZ)),
         in_hbm(north_wind.reshape(CELLS, NZ)),
         in_hbm(up_wind.reshape(CELLS, NZ)),
@@ -509,7 +526,7 @@
         ],
         compiler_params=pltpu.CompilerParams(vmem_limit_bytes=32 * 1024 * 1024),
         cost_estimate=pl.CostEstimate(flops=2_000_000, bytes_accessed=4_000_000, transcendentals=0),
-    )(*parts)
+    )(parts[0].reshape(2, CELLS, NZ), *parts[1:])
     return result.reshape(2, CX, CY, NZ)
 
 

time: 37.7 us -> 37.3 us (0.989)
  Pallas kernels: 37.6 us -> 37.2 us
    pallas_call x1, Pallas kernels: 35.7 us -> 35.3 us  [body(): pl.pallas_call(functools.partial(kernel, n_x, n_y), out_shape=[jax.ShapeD...]
where the time goes in v9:
time: 37.3 us; the launch traced here: 37.2 us
  Pallas kernels  37.2 us (100%)
    pallas_call x1, Pallas kernels, body(): pl.pallas_call(functools.partial(kernel, n_x, n_y), out_shape=[jax.ShapeD...  35.3 us
    pallas_call x1, Pallas kernels, body(): pl.pallas_call(solve, out_shape=jax.ShapeDtypeStruct((2, CELLS, NZ), f32)...  1.95 us

profile of v9, /device:TPU:1, one launch (start us, length us, event | category | flops | bytes accessed | tf_op | source)
XLA Modules:
  0.0 37.2 jit_solution(8429349832617593613)
XLA Ops:
  0.0 35.3 %shard_map.64 = (f32[2,24,32,128]{3,2,1,0:T(8,128)S(1)}, f32[2,128]{1,0:T(2,128)S(1)}, f32[1152,128]{1,0:T(8,128)S(1)}, f32[1152,128]{1,0:T(8,128)S(1)}, f32[1152,128]{1,0:T(8,128)S(1)}) custom-call(f32[2,24,32,128]{3,2,1,0:T(8,128)} %scal.1, f32[768,128]{1,0:T(8,128)} %bitcast.7, f32[768,128]{1,0:T(8,128)} %bitcast.8, f32[768,128]{1,0:T(8,128)} %bitcast.9, ...), custom_call_target="tpu_custom_call" | custom-call | flops 80000000 | bytes 4000000 | tf_op jit(solution)/shard_map/pallas_call | solution.py:472
  35.3 2.0 %shard_map.65 = f32[2,768,128]{2,1,0:T(8,128)} custom-call(f32[2,768,128]{2,1,0:T(8,128)S(1)} %bitcast.6, f32[2,128]{1,0:T(2,128)S(1)} %get-tuple-element.11.shift, f32[1152,128]{1,0:T(8,128)S(1)} %get-tuple-element.12.im, f32[1152,128]{1,0:T(8,128)S(1)} %get-tuple-element.13.av, f32[1152,128]{1,0:T(8,128)S(1)} %get-tuple-element.14.cp), custom_call_target="tpu_custom_call" | custom-call | flops 2000000 | bytes 4000000 | tf_op jit(solution)/shard_map/pallas_call | solution.py:517

commit v10 on v9

--- a/solution.py
+++ b/solution.py
@@ -336,7 +336,7 @@
 
         lax.fori_loop(0, 2, z_pass, 0)
 
-        @pl.when(st < rounds - 1)
+        @pl.when(st < min(2, rounds - 1))
         def _():
             add_sums(st)
             send_sums(st + 1)
@@ -388,6 +388,13 @@
             return 0
 
         lax.fori_loop(0, 2, finish, 0)
+        if rounds > 3:
+
+            @pl.when(st == 1)
+            def _():
+                add_sums(2)
+                send_sums(3)
+
         return 0
 
     lax.fori_loop(0, 3, stage, 0)

time: 37.3 us -> 36.9 us (0.989)
  Pallas kernels: 37.2 us -> 36.8 us
    pallas_call x1, Pallas kernels: 35.3 us -> 34.8 us  [body(): pl.pallas_call(functools.partial(kernel, n_x, n_y), out_shape=[jax.ShapeD...]
where the time goes in v10:
time: 36.9 us; the launch traced here: 36.8 us
  Pallas kernels  36.8 us (100%)
    pallas_call x1, Pallas kernels, body(): pl.pallas_call(functools.partial(kernel, n_x, n_y), out_shape=[jax.ShapeD...  34.8 us
    pallas_call x1, Pallas kernels, body(): pl.pallas_call(solve, out_shape=jax.ShapeDtypeStruct((2, CELLS, NZ), f32)...  1.95 us

profile of v10, /device:TPU:1, one launch (start us, length us, event | category | flops | bytes accessed | tf_op | source)
XLA Modules:
  0.0 36.8 jit_solution(14009425021821372658)
XLA Ops:
  0.0 34.8 %shard_map.64 = (f32[2,24,32,128]{3,2,1,0:T(8,128)S(1)}, f32[2,128]{1,0:T(2,128)S(1)}, f32[1152,128]{1,0:T(8,128)S(1)}, f32[1152,128]{1,0:T(8,128)S(1)}, f32[1152,128]{1,0:T(8,128)S(1)}) custom-call(f32[2,24,32,128]{3,2,1,0:T(8,128)} %scal.1, f32[768,128]{1,0:T(8,128)} %bitcast.7, f32[768,128]{1,0:T(8,128)} %bitcast.8, f32[768,128]{1,0:T(8,128)} %bitcast.9, ...), custom_call_target="tpu_custom_call" | custom-call | flops 80000000 | bytes 4000000 | tf_op jit(solution)/shard_map/pallas_call | solution.py:479
  34.8 2.0 %shard_map.65 = f32[2,768,128]{2,1,0:T(8,128)} custom-call(f32[2,768,128]{2,1,0:T(8,128)S(1)} %bitcast.6, f32[2,128]{1,0:T(2,128)S(1)} %get-tuple-element.11.shift, f32[1152,128]{1,0:T(8,128)S(1)} %get-tuple-element.12.im, f32[1152,128]{1,0:T(8,128)S(1)} %get-tuple-element.13.av, f32[1152,128]{1,0:T(8,128)S(1)} %get-tuple-element.14.cp), custom_call_target="tpu_custom_call" | custom-call | flops 2000000 | bytes 4000000 | tf_op jit(solution)/shard_map/pallas_call | solution.py:524

commit v11 on v10

--- a/solution.py
+++ b/solution.py
@@ -21,8 +21,8 @@
 GROUP = 8
 ZROWS = 192
 TURN = 16
-PART = 48
-LEVELS = 3 * PART
+PART = 64
+LEVELS = 2 * PART
 UNROLL = PART // 8
 MESH = pl.DeviceIdType.MESH
 
@@ -250,19 +250,28 @@
     loads[5].wait()
     lane = lax.broadcasted_iota(jnp.int32, (8, NZ), 1)
 
-    loads[4].wait()
     loads[6].wait()
     loads[7].wait()
-
-    def columns_to_lanes(c, _):
-        rows = pl.ds(pl.multiple_of(c * 128, 128), 128)
-        fk[pl.ds(c, NZ, stride=8), :] = jnp.transpose(kd[rows, :]) * STEP
+    es[...] = jnp.zeros((8, 128), jnp.float32)
+    clear = 16
+
+    def zero_factors(i, _):
+        fk[pl.ds(pl.multiple_of(i * (clear * 8), 8), clear * 8), :] = jnp.zeros((clear * 8, 128), jnp.float32)
         return 0
 
-    fk[pl.ds(NZ * 8, fk.shape[0] - NZ * 8), :] = jnp.zeros((fk.shape[0] - NZ * 8, 128), jnp.float32)
-    lax.fori_loop(0, TILES, columns_to_lanes, 0)
-    fk[pl.ds(0, 8), :] = jnp.zeros((8, 128), jnp.float32)
-    es[...] = jnp.zeros((8, 128), jnp.float32)
+    lax.fori_loop(0, NZ // clear, zero_factors, 0)
+    fk[pl.ds(NZ * 8, 8), :] = jnp.zeros((8, 128), jnp.float32)
+
+    def start_factors():
+        def columns_to_lanes(c, _):
+            rows = pl.ds(pl.multiple_of(c * 128, 128), 128)
+            fk[pl.ds(c, NZ, stride=8), :] = jnp.transpose(kd[rows, :]) * STEP
+            return 0
+
+        loads[4].wait()
+        lax.fori_loop(0, TILES, columns_to_lanes, 0)
+        fk[pl.ds(0, 8), :] = jnp.zeros((8, 128), jnp.float32)
+        es[...] = jnp.zeros((8, 128), jnp.float32)
 
     def factor(first, e):
         base = pl.multiple_of(first * 8, 8)
@@ -346,6 +355,10 @@
             north_edge.wait_recv()
             east_edge.wait_recv()
 
+        @pl.when(st == 1)
+        def _():
+            start_factors()
+
         def finish(s, _):
             t = 2 * st + s
 
@@ -356,7 +369,7 @@
             def x_pass(i, e):
                 row = pl.multiple_of(i * 8, 8)
                 x_column(st, s, row, coef)
-                e = factor(st * PART + (s * (CY // 8) + i) * UNROLL, e)
+                e = factor(lax.max(st - 1, 0) * PART + (s * (CY // 8) + i) * UNROLL, e)
 
                 @pl.when(st < 2)
                 def _():

time: 36.9 us -> 37.9 us (1.027)
  Pallas kernels: 36.8 us -> 37.8 us
    pallas_call x1, Pallas kernels: 34.8 us -> 35.9 us  [body(): pl.pallas_call(functools.partial(kernel, n_x, n_y), out_shape=[jax.ShapeD...]
where the time goes in v11:
time: 37.9 us
  Pallas kernels  37.8 us (100%)
    pallas_call x1, Pallas kernels, body(): pl.pallas_call(functools.partial(kernel, n_x, n_y), out_shape=[jax.ShapeD...  35.9 us
    pallas_call x1, Pallas kernels, body(): pl.pallas_call(solve, out_shape=jax.ShapeDtypeStruct((2, CELLS, NZ), f32)...  1.95 us

profile of v11, /device:TPU:1, one launch (start us, length us, event | category | flops | bytes accessed | tf_op | source)
XLA Modules:
  0.0 37.9 jit_solution(3128045068499348329)
XLA Ops:
  0.0 35.9 %shard_map.64 = (f32[2,24,32,128]{3,2,1,0:T(8,128)S(1)}, f32[2,128]{1,0:T(2,128)S(1)}, f32[1024,128]{1,0:T(8,128)S(1)}, f32[1024,128]{1,0:T(8,128)S(1)}, f32[1024,128]{1,0:T(8,128)S(1)}) custom-call(f32[2,24,32,128]{3,2,1,0:T(8,128)} %scal.1, f32[768,128]{1,0:T(8,128)} %bitcast.7, f32[768,128]{1,0:T(8,128)} %bitcast.8, f32[768,128]{1,0:T(8,128)} %bitcast.9, ...), custom_call_target="tpu_custom_call" | custom-call | flops 80000000 | bytes 4000000 | tf_op jit(solution)/shard_map/pallas_call | solution.py:492
  35.9 2.0 %shard_map.65 = f32[2,768,128]{2,1,0:T(8,128)} custom-call(f32[2,768,128]{2,1,0:T(8,128)S(1)} %bitcast.6, f32[2,128]{1,0:T(2,128)S(1)} %get-tuple-element.11.shift, f32[1024,128]{1,0:T(8,128)S(1)} %get-tuple-element.12.im, f32[1024,128]{1,0:T(8,128)S(1)} %get-tuple-element.13.av, f32[1024,128]{1,0:T(8,128)S(1)} %get-tuple-element.14.cp), custom_call_target="tpu_custom_call" | custom-call | flops 2000000 | bytes 4000000 | tf_op jit(solution)/shard_map/pallas_call | solution.py:537

commit v12 on v10

--- a/solution.py
+++ b/solution.py
@@ -264,20 +264,22 @@
     fk[pl.ds(0, 8), :] = jnp.zeros((8, 128), jnp.float32)
     es[...] = jnp.zeros((8, 128), jnp.float32)
 
-    def factor(first, e):
+    def factor_levels(first, e):
         base = pl.multiple_of(first * 8, 8)
-        low = fk[pl.ds(base, 8), :]
-        for i in range(UNROLL):
+        state = {"e": e, "low": fk[pl.ds(base, 8), :]}
+
+        def level(i):
             row = pl.ds(base + 8 * i, 8)
+            low = state["low"]
             above = fk[pl.ds(base + 8 * i + 8, 8), :]
-            g = 1.0 + low * e
+            g = 1.0 + low * state["e"]
             inverse = pl.reciprocal(g + above, approx=True)
-            e = g * inverse
             im[row, :] = inverse
             av[row, :] = low * inverse
             cp[row, :] = above * inverse
-            low = above
-        return e
+            state["e"], state["low"] = g * inverse, above
+
+        return state, level
 
     def y_column(st, s, row):
         def keep(y, diff):
@@ -289,7 +291,7 @@
             CY, keep,
         )
 
-    def x_column(st, s, row, coef):
+    def x_column(st, s, row, coef, level):
         t = 2 * st + s
 
         def load(x):
@@ -304,6 +306,8 @@
             value = bs[s, x, pl.ds(row, 8), :] + coef * (diff + ty[rows, :] + tz[s, rows, :])
             adv[s, x, pl.ds(row, 8), :] = value
             ys[st + 1, s, pl.ds((H + row) * CX + x, 8, stride=CX), :] = value
+            if x % 4 == 3:
+                level(x // 4)
 
         march(load, lambda x: ex[pl.ds(x * CY + row, 8), :], CX, keep)
 
@@ -355,8 +359,9 @@
 
             def x_pass(i, e):
                 row = pl.multiple_of(i * 8, 8)
-                x_column(st, s, row, coef)
-                e = factor(st * PART + (s * (CY // 8) + i) * UNROLL, e)
+                state, level = factor_levels(st * PART + (s * (CY // 8) + i) * UNROLL, e)
+                x_column(st, s, row, coef, level)
+                e = state["e"]
 
                 @pl.when(st < 2)
                 def _():

time: 36.9 us -> 36.7 us (level)
  no operation moved by 1% of the time
where the time goes in v12:
time: 36.7 us
  Pallas kernels  36.6 us (100%)
    pallas_call x1, Pallas kernels, body(): pl.pallas_call(functools.partial(kernel, n_x, n_y), out_shape=[jax.ShapeD...  34.7 us
    pallas_call x1, Pallas kernels, body(): pl.pallas_call(solve, out_shape=jax.ShapeDtypeStruct((2, CELLS, NZ), f32)...  1.95 us

profile of v12, /device:TPU:1, one launch (start us, length us, event | category | flops | bytes accessed | tf_op | source)
XLA Modules:
  0.0 36.7 jit_solution(7671876808916464912)
XLA Ops:
  0.0 34.7 %shard_map.64 = (f32[2,24,32,128]{3,2,1,0:T(8,128)S(1)}, f32[2,128]{1,0:T(2,128)S(1)}, f32[1152,128]{1,0:T(8,128)S(1)}, f32[1152,128]{1,0:T(8,128)S(1)}, f32[1152,128]{1,0:T(8,128)S(1)}) custom-call(f32[2,24,32,128]{3,2,1,0:T(8,128)} %scal.1, f32[768,128]{1,0:T(8,128)} %bitcast.7, f32[768,128]{1,0:T(8,128)} %bitcast.8, f32[768,128]{1,0:T(8,128)} %bitcast.9, ...), custom_call_target="tpu_custom_call" | custom-call | flops 80000000 | bytes 4000000 | tf_op jit(solution)/shard_map/pallas_call | solution.py:484
  34.7 2.0 %shard_map.65 = f32[2,768,128]{2,1,0:T(8,128)} custom-call(f32[2,768,128]{2,1,0:T(8,128)S(1)} %bitcast.6, f32[2,128]{1,0:T(2,128)S(1)} %get-tuple-element.11.shift, f32[1152,128]{1,0:T(8,128)S(1)} %get-tuple-element.12.im, f32[1152,128]{1,0:T(8,128)S(1)} %get-tuple-element.13.av, f32[1152,128]{1,0:T(8,128)S(1)} %get-tuple-element.14.cp), custom_call_target="tpu_custom_call" | custom-call | flops 2000000 | bytes 4000000 | tf_op jit(solution)/shard_map/pallas_call | solution.py:529
